TPU v7x, 512 devices: a whole 4x4x16 slice. The times are simulated.
512 devices in a mesh: row: 32 (over x, z_lo, core), col: 16 (over z_hi, y).
Axes of the slice: x: 4, y: 4, z: 16 (z_hi: 4, z_lo: 4; z = z_hi * 4 + z_lo), core: 2. Of those that a mesh axis runs over, the one named last changes fastest.
Arguments:
- transmission: float32 [2, 2, 2048, 4096], P(None, None, 'row', 'col'), may hold values from -0.5 to 1.5
- probe: float32 [2, 128, 128], replicated, may hold values from -6 to 6
- prop_phase: float32 [128, 128], replicated, may hold values from -3.140625 to 3.140625
- intensity: bfloat16 [2048, 128, 128], P(('row', 'col')), may hold values from 0.049804688 to 4
- offsets: int32 [2048, 2], P(('row', 'col')), may hold values from 0 to 256, as said below
- counts: int32 [512], P(('row', 'col')), may hold values from 1 to 4, as said below
Outputs:
- object_grad: float32 [2, 2, 2048, 4096], P(None, None, 'row', 'col')
- probe_grad: float32 [2, 128, 128], replicated
Inputs may be any that keep to these rules, and one draw needn't show every extreme that they name: offsets[q, 0] lies within 0 to 64 and offsets[q, 1] within 0 to 256, so a window lies in its own tile and the 64 cells around it; both ends are reached. `counts`: some device has all 4 slots live.
All inputs are finite; a program needn't handle non-finite values.
Results may differ from a plain program's by a relative error of at most 0.0003.
Values sent between devices are 32-bit elements; how exact they have to be, the bound alone decides.
A program may use at most 64 MiB of HBM per device.

v0:
```python
import math

import jax
import jax.numpy as jnp
from jax import lax
from jax.sharding import PartitionSpec as P


def from_behind(value, axis, steps):
    count = lax.axis_size(axis)
    leading, last = (max(0, -steps), min(count, count - steps))
    return lax.ppermute(value, axis, [(source, source + steps) for source in range(leading, last)])


def padded(cells, sides, width):
    for axis, dim in sides:
        count = lax.axis_size(axis)
        ends = count - 1
        head = lax.slice_in_dim(cells, 0, width, axis=dim)
        tail = lax.slice_in_dim(cells, cells.shape[dim] - width, cells.shape[dim], axis=dim)
        cells = jnp.concatenate(
            [
                lax.ppermute(tail, axis, [(i, (i + 1) % count) for i in range(ends)]),
                cells,
                lax.ppermute(head, axis, [((i + 1) % count, i) for i in range(ends)]),
            ],
            axis=dim,
        )
    return cells


def dft_tables(side):
    index = jnp.arange(side, dtype=jnp.int32)
    product = index[:, None] * index[None, :] % side
    angles = product.astype(jnp.float32) * (-2.0 * math.pi / side)
    factor = 1.0 / math.sqrt(side)
    return (jnp.cos(angles) * factor, jnp.sin(angles) * factor)


def complex_mul(left_re, left_im, right_re, right_im):
    return (left_re * right_re - left_im * right_im, left_re * right_im + left_im * right_re)


def transform(field_re, field_im, table_re, table_im):
    high = lax.Precision.HIGHEST
    step_re = jnp.einsum("jk,kl->jl", field_re, table_re, precision=high) - jnp.einsum(
        "jk,kl->jl", field_im, table_im, precision=high
    )
    step_im = jnp.einsum("jk,kl->jl", field_re, table_im, precision=high) + jnp.einsum(
        "jk,kl->jl", field_im, table_re, precision=high
    )
    out_re = jnp.einsum("jk,kl->jl", table_re, step_re, precision=high) - jnp.einsum(
        "jk,kl->jl", table_im, step_im, precision=high
    )
    out_im = jnp.einsum("jk,kl->jl", table_re, step_im, precision=high) + jnp.einsum(
        "jk,kl->jl", table_im, step_re, precision=high
    )
    return (out_re, out_im)


def slot_loss(probe, patch, measured, propagator, table_re, table_im):
    wave_re, wave_im = (probe[0], probe[1])
    layers = patch.shape[1]
    for layer in range(layers):
        mixed_re, mixed_im = complex_mul(wave_re, wave_im, patch[0, layer], patch[1, layer])
        freq_re, freq_im = transform(mixed_re, mixed_im, table_re, table_im)
        if layer + 1 < layers:
            moved_re, moved_im = complex_mul(freq_re, freq_im, propagator[0], propagator[1])
            wave_re, wave_im = transform(moved_re, moved_im, table_re, -table_im)
    power = freq_re * freq_re + freq_im * freq_im
    return 0.5 * jnp.sum((power - measured) ** 2)


def batch_loss(probe, patches, measured, propagator, weights, table_re, table_im):
    losses = jax.vmap(slot_loss, in_axes=(None, 0, 0, None, None, None))(
        probe, patches, measured, propagator, table_re, table_im
    )
    return jnp.sum(weights * losses)


def fold_rows(grid, margin):
    inner = grid.shape[2] - 2 * margin
    top_rim = grid[:, :, :margin]
    bottom_rim = grid[:, :, inner + margin :]
    from_next = from_behind(top_rim, "row", -1)
    from_prev = from_behind(bottom_rim, "row", 1)
    middle = grid[:, :, margin : margin + inner]
    middle = middle.at[:, :, inner - margin : inner].add(from_next)
    return middle.at[:, :, :margin].add(from_prev)


def fold_cols(grid, margin):
    inner = grid.shape[3] - 2 * margin
    left_rim = grid[:, :, :, :margin]
    right_rim = grid[:, :, :, inner + margin :]
    from_next = from_behind(left_rim, "col", -1)
    from_prev = from_behind(right_rim, "col", 1)
    middle = grid[:, :, :, margin : margin + inner]
    middle = middle.at[:, :, :, inner - margin : inner].add(from_next)
    return middle.at[:, :, :, :margin].add(from_prev)


def shards(transmission, probe, prop_phase, intensity, offsets, counts):
    side = probe.shape[1]
    margin = side // 2
    slots = offsets.shape[0]
    layers = transmission.shape[1]
    table_re, table_im = dft_tables(side)
    propagator = jnp.stack([jnp.cos(prop_phase), jnp.sin(prop_phase)])
    extended = padded(transmission, (("row", 2), ("col", 3)), margin)
    zero = jnp.zeros((), jnp.int32)
    shape = (2, layers, side, side)
    weights = (jnp.arange(slots, dtype=jnp.int32) < counts[0]).astype(jnp.float32)

    def take(offset):
        return lax.dynamic_slice(extended, (zero, zero, offset[0], offset[1]), shape)

    patches = jax.vmap(take)(offsets)
    grad_probe, grad_patch = jax.grad(batch_loss, argnums=(0, 1))(
        probe, patches, intensity.astype(jnp.float32), propagator, weights, table_re, table_im
    )

    def add_one(slot, grid):
        start = (zero, zero, offsets[slot, 0], offsets[slot, 1])
        current = lax.dynamic_slice(grid, start, shape)
        return lax.dynamic_update_slice(grid, current + grad_patch[slot], start)

    grid = lax.fori_loop(0, slots, add_one, jnp.zeros(extended.shape, jnp.float32))
    object_grad = fold_cols(fold_rows(grid, margin), margin)
    total_slots = slots * lax.axis_size("row") * lax.axis_size("col")
    summed = lax.psum(grad_probe, ("row", "col"))
    return (object_grad, summed / math.sqrt(total_slots))


def solution(mesh):
    in_specs = (
        P(None, None, "row", "col"),
        P(),
        P(),
        P(("row", "col"), None, None),
        P(("row", "col"), None),
        P(("row", "col")),
    )
    out_specs = (P(None, None, "row", "col"), P())
    return jax.shard_map(shards, mesh=mesh, in_specs=in_specs, out_specs=out_specs, check_vma=False)
```

profile of v0, /device:TPU:481, one launch (start us, length us, event | category | flops | bytes accessed | tf_op | source)
XLA Modules:
  0.0 631.1 jit_solution(1648366903305900099)
XLA Ops:
  7.2 5.1 collective-permute-start
  12.4 1.9 collective-permute-start.1
  15.9 0.9 slice_bitcast_fusion.1
  16.8 1.1 fusion.368
  18.0 5.0 collective-permute-done.1
  23.2 3.2 collective-permute-start.2
  26.4 8.1 %collective-permute-start.3 = (f32[2,2,192,64]{3,2,1,0:T(8,128)S(1)}, f32[2,2,192,64]{3,2,1,0:T(8,128)S(1)}, u32[]{:S(2)}, u32[]{:S(2)}) collective-permute-start(f32[2,2,192,64]{3,2,1,0:T(8,128)S(1)} %get-tuple-element.193), channel_id=1, source_target_pairs={{1,0},{2,1},{3,2},{4,3},{5,4},{6,5},{7,6},{8,7},{9,8},{10,9},{11,1... | collective-permute-start | bytes 589832 | tf_op jit(solution)/shard_map/ppermute | solution.py:25
  34.5 26.4 %collective-permute-done.2 = f32[2,2,192,64]{3,2,1,0:T(8,128)S(1)} collective-permute-done((f32[2,2,192,64]{3,2,1,0:T(8,128)S(1)}, f32[2,2,192,64]{3,2,1,0:T(8,128)S(1)}, u32[]{:S(2)}, u32[]{:S(2)}) %collective-permute-start.2) | collective-permute-done | bytes 196640 | tf_op jit(solution)/shard_map/ppermute | solution.py:23
  61.4 8.3 %while.21 = (s32[]{:T(128)}, f32[2,2,192,384]{3,2,1,0:T(8,128)S(1)}, s32[4,4]{1,0:T(4,128)S(1)}, f32[4,2,2,128,128]{4,3,0,2,1:T(8,128)S(1)}, s32[]{:T(128)}) while((s32[]{:T(128)}, f32[2,2,192,384]{3,2,1,0:T(8,128)S(1)}, s32[4,4]{1,0:T(4,128)S(1)}, f32[4,2,2,128,128]{4,3,0,2,1:T(8,128)S(1)}, s32[]{:T(128)}) %tuple.92), condition=%wide.while_cond.4, body=%wide.while_body.4.sunk | while | flops 2 | bytes 524421 | solution.py:116
  62.1 1.4 bitcast_dynamic-update-slice_fusion.2
  64.2 1.4 bitcast_dynamic-update-slice_fusion.2
  66.3 1.4 bitcast_dynamic-update-slice_fusion.2
  68.3 1.4 bitcast_dynamic-update-slice_fusion.2
  82.6 9.3 %fusion.92 = f32[128,4,128]{2,0,1:T(8,128)S(1)} fusion(f32[4,128,128]{2,1,0:T(8,128)S(1)} %convolution_add_fusion.13), kind=kOutput, calls=%fused_computation.159 | convolution fusion | flops 100909056 | bytes 524288 | tf_op jit(solution)/shard_map/jvp(vmap(jk,kl->jl))/dot_general | solution.py:55
  93.9 0.8 fusion.59
  95.5 0.8 fusion.5
  103.7 0.9 fusion.2
  112.8 30.9 %while.20 = (s32[]{:T(128)}, f32[2,2,192,384]{3,2,1,0:T(8,128)S(1)}, s32[4,2]{0,1:T(2,128)S(1)}, f32[4,2,2,128,128]{4,3,0,2,1:T(8,128)S(1)}, s32[]{:T(128)}, /*index=5*/s32[]{:T(128)}, s32[]{:T(128)}, s32[]{:T(128)}) while((s32[]{:T(128)}, f32[2,2,192,384]{3,2,1,0:T(8,128)S(1)}, s32[4,2]{0,1:T(2,128)S(1)}, ...), condition=%wide.region_1.2_spmd, body=%wide.region_0.1_spmd.sunk | while | flops 65544 | bytes 1310917 | solution.py:128
  117.4 3.1 dynamic_update_slice.8
  125.2 3.2 dynamic_update_slice.8
  133.0 3.0 dynamic_update_slice.8
  140.7 3.1 dynamic_update_slice.8
  143.9 2.4 collective-permute-start.4
  146.3 10.0 %collective-permute-start.5 = (f32[2,2,64,384]{3,2,1,0:T(8,128)S(1)}, f32[2,2,64,384]{3,2,1,0:T(8,128)S(1)}, u32[]{:S(2)}, u32[]{:S(2)}) collective-permute-start(f32[2,2,64,384]{3,2,1,0:T(8,128)S(1)} %get-tuple-element.189), channel_id=1, source_target_pairs={{0,16},{16,32},{32,48},{48,64},{64,80},{80,96},{96,112},{112,128},... | collective-permute-start | bytes 1179656 | tf_op jit(solution)/shard_map/ppermute | solution.py:12
  157.1 4.1 collective-permute-done.4
  161.2 1.3 collective-permute-done.5
  162.6 8.6 %collective-permute-start.6 = (f32[2,2,64,64]{3,2,1,0:T(8,128)S(1)}, f32[2,2,64,64]{3,2,1,0:T(8,128)S(1)}, u32[]{:S(2)}, u32[]{:S(2)}) collective-permute-start(f32[2,2,64,64]{3,2,1,0:T(8,128)S(1)} %get-tuple-element.201), channel_id=1, source_target_pairs={{1,0},{2,1},{3,2},{4,3},{5,4},{6,5},{7,6},{8,7},{9,8},{10,9},{11,1... | collective-permute-start | bytes 196616 | tf_op jit(solution)/shard_map/ppermute | solution.py:12
  171.3 429.4 %all-reduce.8.cloned.1.call-done = f32[2,128,128]{2,1,0:T(8,128)} async-done(((f32[2,128,128]{2,1,0:T(8,128)}), f32[2,128,128]{2,1,0:T(8,128)}) %all-reduce.8.cloned.1.call-update) | async-done | bytes 131088 | tf_op jit(solution)/shard_map/psum | solution.py:131
  600.6 1.6 broadcast_multiply_fusion
  602.3 2.6 collective-permute-start.7
  605.0 1.0 scatter-add.6
  606.0 16.6 %collective-permute-done.7 = f32[2,2,64,64]{3,2,1,0:T(8,128)S(1)} collective-permute-done((f32[2,2,64,64]{3,2,1,0:T(8,128)S(1)}, f32[2,2,64,64]{3,2,1,0:T(8,128)S(1)}, u32[]{:S(2)}, u32[]{:S(2)}) %collective-permute-start.7) | collective-permute-done | bytes 65568 | tf_op jit(solution)/shard_map/ppermute | solution.py:12
  (99 shorter events, 40.6 us)
Async XLA Ops:
  7.2 10.8 %copy-start.2 = (f32[2,2,64,256]{3,2,1,0:T(8,128)S(1)}, f32[2,2,64,256]{3,2,1,0:T(8,128)}, u32[]{:S(2)}) copy-start(f32[2,2,64,256]{3,2,1,0:T(8,128)} %param.20) | copy-start | bytes 786436
  7.2 593.5 %all-reduce.8.cloned.1.call-start = ((), (), s32[]{:S(2)}) async-start(), calls=%async_computation | async-start | bytes 262144 | tf_op jit(solution)/shard_map/psum | solution.py:131
  7.2 10.7 %collective-permute-start = (f32[2,2,64,256]{3,2,1,0:T(8,128)}, f32[2,2,64,256]{3,2,1,0:T(8,128)S(1)}, u32[]{:S(2)}, u32[]{:S(2)}) collective-permute-start(f32[2,2,64,256]{3,2,1,0:T(8,128)} %param.20), channel_id=1, source_target_pairs={{0,16},{16,32},{32,48},{48,64},{64,80},{80,96},{96,112},{112,128},... | collective-permute-start | bytes 786440 | tf_op jit(solution)/shard_map/ppermute | solution.py:23
  12.4 10.6 %collective-permute-start.1 = (f32[2,2,64,256]{3,2,1,0:T(8,128)}, f32[2,2,64,256]{3,2,1,0:T(8,128)S(1)}, u32[]{:S(2)}, u32[]{:S(2)}) collective-permute-start(f32[2,2,64,256]{3,2,1,0:T(8,128)} %param.20), channel_id=1, source_target_pairs={{16,0},{32,16},{48,32},{64,48},{80,64},{96,80},{112,96},{128,112},... | collective-permute-start | bytes 786440 | tf_op jit(solution)/shard_map/ppermute | solution.py:25
  23.2 37.8 %collective-permute-start.2 = (f32[2,2,192,64]{3,2,1,0:T(8,128)S(1)}, f32[2,2,192,64]{3,2,1,0:T(8,128)S(1)}, u32[]{:S(2)}, u32[]{:S(2)}) collective-permute-start(f32[2,2,192,64]{3,2,1,0:T(8,128)S(1)} %get-tuple-element.192), channel_id=1, source_target_pairs={{0,1},{1,2},{2,3},{3,4},{4,5},{5,6},{6,7},{7,8},{8,9},{9,10},{10,1... | collective-permute-start | bytes 589832 | tf_op jit(solution)/shard_map/ppermute | solution.py:23
  26.4 34.6 %collective-permute-start.3 = (f32[2,2,192,64]{3,2,1,0:T(8,128)S(1)}, f32[2,2,192,64]{3,2,1,0:T(8,128)S(1)}, u32[]{:S(2)}, u32[]{:S(2)}) collective-permute-start(f32[2,2,192,64]{3,2,1,0:T(8,128)S(1)} %get-tuple-element.193), channel_id=1, source_target_pairs={{1,0},{2,1},{3,2},{4,3},{5,4},{6,5},{7,6},{8,7},{9,8},{10,9},{11,1... | collective-permute-start | bytes 589832 | tf_op jit(solution)/shard_map/ppermute | solution.py:25
  91.9 2.0 copy-start
  112.2 0.7 copy-start.3
  143.9 17.3 %collective-permute-start.4 = (f32[2,2,64,384]{3,2,1,0:T(8,128)S(1)}, f32[2,2,64,384]{3,2,1,0:T(8,128)S(1)}, u32[]{:S(2)}, u32[]{:S(2)}) collective-permute-start(f32[2,2,64,384]{3,2,1,0:T(8,128)S(1)} %get-tuple-element.188), channel_id=1, source_target_pairs={{16,0},{32,16},{48,32},{64,48},{80,64},{96,80},{112,96},{128,112},... | collective-permute-start | bytes 1179656 | tf_op jit(solution)/shard_map/ppermute | solution.py:12
  146.3 16.2 %collective-permute-start.5 = (f32[2,2,64,384]{3,2,1,0:T(8,128)S(1)}, f32[2,2,64,384]{3,2,1,0:T(8,128)S(1)}, u32[]{:S(2)}, u32[]{:S(2)}) collective-permute-start(f32[2,2,64,384]{3,2,1,0:T(8,128)S(1)} %get-tuple-element.189), channel_id=1, source_target_pairs={{0,16},{16,32},{32,48},{48,64},{64,80},{80,96},{96,112},{112,128},... | collective-permute-start | bytes 1179656 | tf_op jit(solution)/shard_map/ppermute | solution.py:12
  162.6 442.3 %collective-permute-start.6 = (f32[2,2,64,64]{3,2,1,0:T(8,128)S(1)}, f32[2,2,64,64]{3,2,1,0:T(8,128)S(1)}, u32[]{:S(2)}, u32[]{:S(2)}) collective-permute-start(f32[2,2,64,64]{3,2,1,0:T(8,128)S(1)} %get-tuple-element.201), channel_id=1, source_target_pairs={{1,0},{2,1},{3,2},{4,3},{5,4},{6,5},{7,6},{8,7},{9,8},{10,9},{11,1... | collective-permute-start | bytes 196616 | tf_op jit(solution)/shard_map/ppermute | solution.py:12
  602.3 20.3 %collective-permute-start.7 = (f32[2,2,64,64]{3,2,1,0:T(8,128)S(1)}, f32[2,2,64,64]{3,2,1,0:T(8,128)S(1)}, u32[]{:S(2)}, u32[]{:S(2)}) collective-permute-start(f32[2,2,64,64]{3,2,1,0:T(8,128)S(1)} %get-tuple-element.200), channel_id=1, source_target_pairs={{0,1},{1,2},{2,3},{3,4},{4,5},{5,6},{6,7},{7,8},{8,9},{9,10},{10,1... | collective-permute-start | bytes 196616 | tf_op jit(solution)/shard_map/ppermute | solution.py:12
  623.1 0.7 copy-start.1
Sparse Core Ops, SparseCore 0:
  157.2 443.4 all-reduce.7
where the time goes:
time: 642 us; the launch traced here: 631 us
  waiting for transfers between devices  483 us (75%)
  starting transfers between devices  42.1 us (7%)
  matrix products  42 us (7%)
  local copies, waits for them, and re-layouts  29.3 us (5%)
  between operations  15.7 us (2%)
  loops' own time  15.6 us (2%)
    psum x1, waiting for transfers between devices, shards(): summed = lax.psum(grad_probe, ('row', 'col'))  429 us
    ppermute x2, waiting for transfers between devices, padded(): lax.ppermute(tail, axis, [(i, (i + 1) % count) for i in range(ends)])  26.4 us
    ppermute x4, starting transfers between devices, from_behind(): lax.ppermute(value, axis, [(source, source + steps) for source in range(l...  23.7 us
    ppermute x4, waiting for transfers between devices, from_behind(): lax.ppermute(value, axis, [(source, source + steps) for source in range(l...  22.1 us
    another operation x1, loops' own time, shards(): lax.fori_loop(0, slots, add_one, jnp.zeros(extended.shape, jnp.float32))  15.4 us
    dot_general x6, matrix products, transform(): jnp.einsum('jk,kl->jl', table_re, step_im, precision=high)  12.9 us
  transfers between devices with their start and end apart: 9, of which 6 were waited for; matrix products, arithmetic and copies ran while one was open for 1% of the time, Pallas kernels for 0%

commit v1 on v0

v1 whole, which is shorter than its diff:
```python
import functools
import math

import jax
import jax.numpy as jnp
import ml_dtypes
import numpy as np
from jax import lax
from jax.experimental import pallas as pl
from jax.experimental.pallas import tpu as pltpu
from jax.sharding import PartitionSpec as P

MESH = pl.DeviceIdType.MESH
SIDE = 128
HALF = 64
TILES = 3


def dft_tables():
    index = np.arange(SIDE)
    angles = (index[:, None] * index[None, :] % SIDE) * (-2.0 * math.pi / SIDE)
    re, im = np.cos(angles) / math.sqrt(SIDE), np.sin(angles) / math.sqrt(SIDE)
    wide = np.block([[re, im], [-im, re]])
    parts = []
    for table in (wide, wide.T):
        high = table.astype(ml_dtypes.bfloat16)
        parts += [high, (table - high.astype(np.float64)).astype(ml_dtypes.bfloat16)]
    return np.stack(parts)


def halves(value):
    high = value.astype(jnp.bfloat16)
    return high, (value - high.astype(jnp.float32)).astype(jnp.bfloat16)


def product(left, right):
    dot = functools.partial(jnp.dot, preferred_element_type=jnp.float32)
    return dot(left[0], right[0]) + dot(left[1], right[0]) + dot(left[0], right[1])


def along_lanes(re, im, table):
    out = product(halves(jnp.concatenate([re, im], axis=1)), table)
    return out[:, :SIDE], out[:, SIDE:]


def along_rows(re, im, table):
    slots = re.shape[0] // SIDE
    beside = lambda part: jnp.concatenate([part[s * SIDE : (s + 1) * SIDE] for s in range(slots)], axis=1)
    out = product(table, halves(jnp.concatenate([beside(re), beside(im)], axis=0)))
    below = lambda part: jnp.concatenate([part[:, s * SIDE : (s + 1) * SIDE] for s in range(slots)], axis=0)
    return below(out[:SIDE]), below(out[SIDE:])


def times(a_re, a_im, b_re, b_im):
    return a_re * b_re - a_im * b_im, a_re * b_im + a_im * b_re


def times_conj(a_re, a_im, b_re, b_im):
    return a_re * b_re + a_im * b_im, a_im * b_re - a_re * b_im


def remote(src, dst, send, recv, device):
    return pltpu.make_async_remote_copy(
        src_ref=src, dst_ref=dst, send_sem=send, recv_sem=recv, device_id=device, device_id_type=MESH
    )


def kernel(
    rows, cols, total_slots,
    offsets, counts, trans, probe_in, phase_in, intensity_in, tables_in,
    object_out, probe_out,
    ext_first, ext_second, probe, phase, intensity, tables, edge_out, edge_in, patch, wave, prop, place, grid, fold_in, rim_out, rim_in,
    sum_out, sum_in, col_in, gathered,
    load_sem, edge_send, edge_recv, row_send, row_recv, fold_send, fold_recv, rim_send, rim_recv, sum_send, sum_recv,
):
    ext = (ext_first, ext_second)
    slots = intensity.shape[0]
    row, col = lax.axis_index("row"), lax.axis_index("col")
    up, down = lax.rem(row + rows - 1, rows), lax.rem(row + 1, rows)
    left, right = lax.rem(col + cols - 1, cols), lax.rem(col + 1, cols)
    lane = lax.broadcasted_iota(jnp.int32, (HALF, SIDE), 1)
    low = lane < HALF
    own = slice(HALF, 2 * HALF)

    own_loads = [
        [
            pltpu.make_async_copy(
                trans.at[:, layer, :, pl.ds(tile * SIDE, SIDE)], ext[layer].at[:, tile, own, :], load_sem.at[layer * 2 + tile]
            )
            for tile in range(2)
        ]
        for layer in range(2)
    ]
    small_loads = [
        pltpu.make_async_copy(src, dst, load_sem.at[4 + i])
        for i, (src, dst) in enumerate(
            [(phase_in, phase), (probe_in, probe), (tables_in, tables), (intensity_in, intensity)]
        )
    ]
    for layer in own_loads:
        for copy in layer:
            copy.start()
    for copy in small_loads:
        copy.start()

    barrier = pltpu.get_barrier_semaphore()

    def greet_row(k, _):
        pl.semaphore_signal(barrier, inc=1, device_id={"row": lax.rem(row + k, rows)}, device_id_type=MESH)
        return 0

    def greet_col(k, _):
        pl.semaphore_signal(barrier, inc=1, device_id={"col": lax.rem(col + k, cols)}, device_id_type=MESH)
        return 0

    lax.fori_loop(1, rows, greet_row, 0)
    lax.fori_loop(1, cols, greet_col, 0)
    pl.semaphore_wait(barrier, rows + cols - 2)

    def edge_copies(layer):
        return [
            remote(edge_out.at[layer, 0], edge_in.at[layer, 0], edge_send.at[layer, 0], edge_recv.at[layer, 0], {"col": right}),
            remote(edge_out.at[layer, 1], edge_in.at[layer, 1], edge_send.at[layer, 1], edge_recv.at[layer, 1], {"col": left}),
        ]

    def row_copies(layer, part):
        tiles = slice(0, 2) if part == 0 else slice(2, 3)
        src = ext[layer].at[:, tiles, own, :]
        return [
            remote(
                src, ext[layer].at[:, tiles, 0:HALF, :],
                row_send.at[layer, part, 0], row_recv.at[layer, part, 0], {"row": down},
            ),
            remote(
                src, ext[layer].at[:, tiles, 2 * HALF : 3 * HALF, :],
                row_send.at[layer, part, 1], row_recv.at[layer, part, 1], {"row": up},
            ),
        ]

    def start(copies):
        for copy in copies:
            copy.start()

    def landed(copies):
        for copy in copies:
            copy.wait_recv()

    def sent(copies):
        for copy in copies:
            copy.wait_send()

    for layer in range(2):
        for copy in own_loads[layer]:
            copy.wait()
        edge_out[layer, 0] = jnp.where(
            low, pltpu.roll(ext[layer][1, 1, own, :], HALF, 1), ext[layer][0, 1, own, :]
        )
        edge_out[layer, 1] = jnp.where(
            low, ext[layer][0, 0, own, :], pltpu.roll(ext[layer][1, 0, own, :], HALF, 1)
        )
        start(edge_copies(layer))
        start(row_copies(layer, 0))

    for layer in range(2):
        landed(edge_copies(layer))
        from_left = jnp.where(col > 0, edge_in[layer, 0], 0.0)
        from_right = jnp.where(col < cols - 1, edge_in[layer, 1], 0.0)
        ext[layer][0, 2, own, :] = jnp.where(low, from_right, from_left)
        ext[layer][1, 2, own, :] = pltpu.roll(jnp.where(low, from_left, from_right), HALF, 1)
        start(row_copies(layer, 1))

    place[:, :, :, 0:2, 0:HALF, :] = jnp.zeros(place.shape[:3] + (2, HALF, SIDE), jnp.float32)
    place[:, :, :, 0:2, 3 * HALF :, :] = jnp.zeros(place.shape[:3] + (2, HALF, SIDE), jnp.float32)
    place[:, :, :, 2, :, :] = jnp.zeros(place.shape[:3] + (4 * HALF, SIDE), jnp.float32)
    for copy in small_loads:
        copy.wait()
    prop[0] = jnp.cos(phase[...])
    prop[1] = jnp.sin(phase[...])

    lanes = lax.broadcasted_iota(jnp.int32, (SIDE, SIDE), 1)

    def spot(slot):
        across = offsets[slot, 1] + (TILES * SIDE - HALF)
        tile = lax.rem(lax.div(across, SIDE), TILES)
        return offsets[slot, 0], tile, lax.rem(tile + 1, TILES), lax.rem(across, SIDE)

    spots = [spot(slot) for slot in range(slots)]

    def rows_arrived(layer):
        landed(row_copies(layer, 0))
        landed(row_copies(layer, 1))

        @pl.when(row == 0)
        def _():
            ext[layer][:, :, 0:HALF, :] = jnp.zeros((2, TILES, HALF, SIDE), jnp.float32)

        @pl.when(row == rows - 1)
        def _():
            ext[layer][:, :, 2 * HALF :, :] = jnp.zeros((2, TILES, HALF, SIDE), jnp.float32)

    def gather(layer):
        for slot, (top, tile, after, shift) in enumerate(spots):
            back = lax.rem(SIDE - shift, SIDE)
            for part in range(2):
                first = ext[layer][part, tile, pl.ds(top, SIDE), :]
                second = ext[layer][part, after, pl.ds(top, SIDE), :]
                patch[layer, part, slot * SIDE : (slot + 1) * SIDE, :] = pltpu.roll(
                    jnp.where(lanes < shift, second, first), back, 1
                )

    def scatter(layer, grad):
        for slot, (_, _, _, shift) in enumerate(spots):
            for part in range(2):
                moved = pltpu.roll(grad[part][slot * SIDE : (slot + 1) * SIDE], shift, 1)
                place[layer, part, slot, 0, HALF : 3 * HALF, :] = jnp.where(lanes < shift, 0.0, moved)
                place[layer, part, slot, 1, HALF : 3 * HALF, :] = jnp.where(lanes < shift, moved, 0.0)
        for tile in reversed(range(TILES)):
            for part in range(2):
                total = None
                for slot, (top, first, second, _) in enumerate(spots):
                    which = jnp.where(first == tile, 0, jnp.where(second == tile, 1, 2))
                    term = place[layer, part, slot, which, pl.ds(HALF - top, 3 * HALF), :]
                    total = term if total is None else total + term
                grid[layer, part, tile] = total
            if tile == 2:
                start(fold_copies(layer, 1))
        start(fold_copies(layer, 0))

    def fold_copies(layer, part):
        tiles = slice(0, 2) if part == 0 else slice(2, 3)
        return [
            remote(
                grid.at[layer, :, tiles, 2 * HALF : 3 * HALF, :], fold_in.at[layer, 0, :, tiles],
                fold_send.at[layer, part, 0], fold_recv.at[layer, part, 0], {"row": down},
            ),
            remote(
                grid.at[layer, :, tiles, 0:HALF, :], fold_in.at[layer, 1, :, tiles],
                fold_send.at[layer, part, 1], fold_recv.at[layer, part, 1], {"row": up},
            ),
        ]

    def rim_copies(layer):
        return [
            remote(rim_out.at[layer, 0], rim_in.at[layer, 0], rim_send.at[layer, 0], rim_recv.at[layer, 0], {"col": right}),
            remote(rim_out.at[layer, 1], rim_in.at[layer, 1], rim_send.at[layer, 1], rim_recv.at[layer, 1], {"col": left}),
        ]

    repeat = lambda part: jnp.concatenate([part] * slots, axis=0)
    wide = (tables[0], tables[1])
    tall = (tables[2], tables[3])

    def transform(field):
        return along_rows(*along_lanes(*field, wide), tall)

    def inverse(field):
        return along_rows(*along_lanes(*field, tall), wide)

    shone = (repeat(probe[0]), repeat(probe[1]))
    moved = (repeat(prop[0]), repeat(prop[1]))

    rows_arrived(0)
    gather(0)
    field = times(*shone, patch[0, 0], patch[0, 1])
    field = inverse(times(*transform(field), *moved))
    wave[0] = field[0]
    wave[1] = field[1]
    rows_arrived(1)
    gather(1)
    far = transform(times(*field, patch[1, 0], patch[1, 1]))
    live = jnp.concatenate(
        [jnp.full((SIDE, SIDE), jnp.where(slot < counts[0], 2.0, 0.0), jnp.float32) for slot in range(slots)], axis=0
    )
    measured = jnp.concatenate([intensity[slot].astype(jnp.float32) for slot in range(slots)], axis=0)
    excess = (far[0] * far[0] + far[1] * far[1] - measured) * live
    back = inverse((far[0] * excess, far[1] * excess))
    scatter(1, times_conj(*back, wave[0], wave[1]))
    back = transform(times_conj(*back, patch[1, 0], patch[1, 1]))
    back = inverse(times_conj(*back, *moved))
    probe_grad = times_conj(*back, patch[0, 0], patch[0, 1])

    scale = 1.0 / math.sqrt(total_slots)
    for part in range(2):
        acc = probe_grad[part][:SIDE]
        for slot in range(1, slots):
            acc = acc + probe_grad[part][slot * SIDE : (slot + 1) * SIDE]
        sum_out[part * SIDE : (part + 1) * SIDE, :] = acc * scale
    depth = 2 * SIDE // rows
    piece = lambda k: pl.ds(pl.multiple_of(k * depth, depth), depth)

    def scatter_piece(k):
        other = lax.rem(row + k, rows)
        return remote(sum_out.at[piece(other)], sum_in.at[row], sum_send.at[0], sum_recv.at[0], {"row": other})

    def share_piece(k):
        return remote(col_in.at[col], col_in.at[col], sum_send.at[1], sum_recv.at[1], {"col": lax.rem(col + k, cols)})

    def spread_piece(k):
        return remote(
            gathered.at[piece(row)], gathered.at[piece(row)], sum_send.at[2], sum_recv.at[2], {"row": lax.rem(row + k, rows)}
        )

    def start_all(copy, count):
        def go(k, _):
            copy(k).start()
            return 0

        lax.fori_loop(1, count, go, 0)

    def wait_bytes(ref, sem):
        pltpu.make_async_copy(ref, ref, sem).wait()

    start_all(scatter_piece, rows)
    scatter(0, times_conj(*back, *shone))

    wait_bytes(sum_in.at[pl.ds(0, rows - 1)], sum_recv.at[0])
    sum_in[row] = sum_out[piece(row), :]
    col_in[col] = jnp.sum(sum_in[...], axis=0)
    start_all(share_piece, cols)

    def fold(layer, tile, part):
        above = jnp.where(row > 0, fold_in[layer, 0, part, tile], 0.0)
        below = jnp.where(row < rows - 1, fold_in[layer, 1, part, tile], 0.0)
        return grid[layer, part, tile, own, :] + above + below

    for layer in (1, 0):
        landed(fold_copies(layer, 1))
        re, im = fold(layer, 2, 0), fold(layer, 2, 1)
        turned = pltpu.roll(im, HALF, 1)
        rim_out[layer, 0] = jnp.where(low, re, turned)
        rim_out[layer, 1] = jnp.where(low, turned, re)
        start(rim_copies(layer))

    wait_bytes(col_in.at[pl.ds(0, cols - 1)], sum_recv.at[1])
    wait_bytes(col_in.at[pl.ds(0, cols - 1)], sum_send.at[1])
    gathered[piece(row), :] = jnp.sum(col_in[...], axis=0)
    start_all(spread_piece, rows)

    for layer in (1, 0):
        landed(fold_copies(layer, 0))
        landed(rim_copies(layer))
        from_left = jnp.where(col > 0, rim_in[layer, 0], 0.0)
        from_right = jnp.where(col < cols - 1, rim_in[layer, 1], 0.0)
        for part in range(2):
            if part == 1:
                from_left, from_right = pltpu.roll(from_left, HALF, 1), pltpu.roll(from_right, HALF, 1)
            object_out[part, layer, :, 0:SIDE] = fold(layer, 0, part) + jnp.where(low, from_left, 0.0)
            object_out[part, layer, :, SIDE:] = fold(layer, 1, part) + jnp.where(low, 0.0, from_right)

    rest = gathered.at[pl.ds(0, depth * (rows - 1))]
    wait_bytes(rest, sum_recv.at[2])
    for part in range(2):
        probe_out[part] = gathered[part * SIDE : (part + 1) * SIDE, :]

    wait_bytes(sum_in.at[pl.ds(0, rows - 1)], sum_send.at[0])
    wait_bytes(rest, sum_send.at[2])
    for layer in range(2):
        sent(edge_copies(layer))
        sent(rim_copies(layer))
        for part in range(2):
            sent(row_copies(layer, part))
            sent(fold_copies(layer, part))


def solution(mesh):
    rows, cols = mesh.shape["row"], mesh.shape["col"]

    def shards(transmission, probe, prop_phase, intensity, offsets, counts):
        slots = offsets.shape[0]
        tables = jnp.asarray(dft_tables())
        f32 = jnp.float32
        depth = 2 * SIDE // rows
        any_space = pl.BlockSpec(memory_space=pl.ANY)
        smem = pl.BlockSpec(memory_space=pltpu.SMEM)
        vmem = pl.BlockSpec(memory_space=pltpu.VMEM)
        dma = pltpu.SemaphoreType.DMA
        return pl.pallas_call(
            functools.partial(kernel, rows, cols, slots * rows * cols),
            out_shape=(
                jax.ShapeDtypeStruct(transmission.shape, f32),
                jax.ShapeDtypeStruct(probe.shape, f32),
            ),
            in_specs=[smem, smem] + [any_space] * 5,
            out_specs=(vmem, vmem),
            scratch_shapes=[
                pltpu.VMEM((2, TILES, 3 * HALF, SIDE), f32),
                pltpu.VMEM((2, TILES, 3 * HALF, SIDE), f32),
                pltpu.VMEM(probe.shape, f32),
                pltpu.VMEM(prop_phase.shape, f32),
                pltpu.VMEM(intensity.shape, intensity.dtype),
                pltpu.VMEM(tables.shape, tables.dtype),
                pltpu.VMEM((2, 2, HALF, SIDE), f32),
                pltpu.VMEM((2, 2, HALF, SIDE), f32),
                pltpu.VMEM((2, 2, slots * SIDE, SIDE), f32),
                pltpu.VMEM((2, slots * SIDE, SIDE), f32),
                pltpu.VMEM((2, SIDE, SIDE), f32),
                pltpu.VMEM((2, 2, slots, 3, 4 * HALF, SIDE), f32),
                pltpu.VMEM((2, 2, TILES, 3 * HALF, SIDE), f32),
                pltpu.VMEM((2, 2, 2, TILES, HALF, SIDE), f32),
                pltpu.VMEM((2, 2, HALF, SIDE), f32),
                pltpu.VMEM((2, 2, HALF, SIDE), f32),
                pltpu.VMEM((2 * SIDE, SIDE), f32),
                pltpu.VMEM((rows, depth, SIDE), f32),
                pltpu.VMEM((cols, depth, SIDE), f32),
                pltpu.VMEM((2 * SIDE, SIDE), f32),
                dma((8,)),
                dma((2, 2)),
                dma((2, 2)),
                dma((2, 2, 2)),
                dma((2, 2, 2)),
                dma((2, 2, 2)),
                dma((2, 2, 2)),
                dma((2, 2)),
                dma((2, 2)),
                dma((3,)),
                dma((3,)),
            ],
            compiler_params=pltpu.CompilerParams(
                collective_id=0, has_side_effects=True, vmem_limit_bytes=40 * 1024 * 1024
            ),
        )(offsets, counts, transmission, probe, prop_phase, intensity, tables)

    in_specs = (
        P(None, None, "row", "col"),
        P(),
        P(),
        P(("row", "col"), None, None),
        P(("row", "col"), None),
        P(("row", "col")),
    )
    out_specs = (P(None, None, "row", "col"), P())
    return jax.shard_map(shards, mesh=mesh, in_specs=in_specs, out_specs=out_specs, check_vma=False)
```

time: 642 us -> 74.6 us (0.12)
  the two profiles are of different devices: /device:TPU:481 before, /device:TPU:1 now
where the time goes in v1:
time: 74.6 us; the launch traced here: 74.3 us
  Pallas kernels  66.9 us (90%)
  local copies, waits for them, and re-layouts  6.1 us (8%)
  between operations  1.31 us (2%)
    pallas_call x1, Pallas kernels, shards(): pl.pallas_call(functools.partial(kernel, rows, cols, slots * rows * cols)...  66.9 us
    unnamed x15, local copies, waits for them, and re-layouts  6.1 us

profile of v1, /device:TPU:1, one launch (start us, length us, event | category | flops | bytes accessed | tf_op | source)
XLA Modules:
  0.0 74.3 jit_solution(5980305676773500277)
XLA Ops:
  0.6 0.0 copy-start.5
  1.3 0.0 copy-done.5
  1.3 0.1 copy.9.offsets
  1.4 0.0 copy-start
  1.4 1.0 %copy-done = bf16[4,256,256]{2,1,0:T(8,128)(2,1)S(1)} copy-done((bf16[4,256,256]{2,1,0:T(8,128)(2,1)S(1)}, bf16[4,256,256]{2,1,0:T(8,128)(2,1)}, u32[]{:S(2)}) %copy-start) | copy-done | bytes 524312
  2.4 0.0 copy-start.1
  2.4 0.9 %copy-done.1 = f32[2,2,64,256]{3,2,1,0:T(8,128)S(1)} copy-done((f32[2,2,64,256]{3,2,1,0:T(8,128)S(1)}, f32[2,2,64,256]{3,2,1,0:T(8,128)}, u32[]{:S(2)}) %copy-start.1) | copy-done | bytes 262168
  3.4 0.0 copy-start.2
  3.4 0.9 %copy-done.2 = f32[2,128,128]{2,1,0:T(8,128)S(1)} copy-done((f32[2,128,128]{2,1,0:T(8,128)S(1)}, f32[2,128,128]{2,1,0:T(8,128)}, u32[]{:S(2)}) %copy-start.2) | copy-done | bytes 131096
  4.3 0.0 copy-start.3
  4.3 0.9 %copy-done.3 = bf16[4,128,128]{2,1,0:T(8,128)(2,1)S(1)} copy-done((bf16[4,128,128]{2,1,0:T(8,128)(2,1)S(1)}, bf16[4,128,128]{2,1,0:T(8,128)(2,1)}, u32[]{:S(2)}) %copy-start.3) | copy-done | bytes 131096
  5.2 0.0 copy-start.4
  5.2 0.8 %copy-done.4 = f32[128,128]{1,0:T(8,128)S(1)} copy-done((f32[128,128]{1,0:T(8,128)S(1)}, f32[128,128]{1,0:T(8,128)}, u32[]{:S(2)}) %copy-start.4) | copy-done | bytes 65560
  6.0 66.9 %shard_map.86 = (f32[2,2,64,256]{3,2,1,0:T(8,128)S(1)}, f32[2,128,128]{2,1,0:T(8,128)S(1)}) custom-call(s32[4,2]{1,0:T(4,128)S(1)} %copy.9.offsets, s32[1]{0:T(128)S(6)} %copy.12.counts, f32[2,2,64,256]{3,2,1,0:T(8,128)S(1)} %copy-done.1, f32[2,128,128]{2,1,0:T(8,128)S(1)} %copy-done.2, f32[128,128]{1,0:T(8,128)S(1)} %copy-done.4, ...), custom_call_target="tpu_custom_call" | custom-call | tf_op jit(solution)/shard_map/pallas_call | solution.py:376
  73.0 0.7 copy.13
  73.7 0.7 copy.14
Async XLA Ops:
  0.6 0.7 copy-start.5
  1.4 1.0 %copy-start = (bf16[4,256,256]{2,1,0:T(8,128)(2,1)S(1)}, bf16[4,256,256]{2,1,0:T(8,128)(2,1)}, u32[]{:S(2)}) copy-start(bf16[4,256,256]{2,1,0:T(8,128)(2,1)} %constant.2.clone.tables_in) | copy-start | bytes 1572868
  2.4 0.9 %copy-start.1 = (f32[2,2,64,256]{3,2,1,0:T(8,128)S(1)}, f32[2,2,64,256]{3,2,1,0:T(8,128)}, u32[]{:S(2)}) copy-start(f32[2,2,64,256]{3,2,1,0:T(8,128)} %trans.1) | copy-start | bytes 786436
  3.4 0.9 %copy-start.2 = (f32[2,128,128]{2,1,0:T(8,128)S(1)}, f32[2,128,128]{2,1,0:T(8,128)}, u32[]{:S(2)}) copy-start(f32[2,128,128]{2,1,0:T(8,128)} %probe_in.1) | copy-start | bytes 393220
  4.3 0.9 %copy-start.3 = (bf16[4,128,128]{2,1,0:T(8,128)(2,1)S(1)}, bf16[4,128,128]{2,1,0:T(8,128)(2,1)}, u32[]{:S(2)}) copy-start(bf16[4,128,128]{2,1,0:T(8,128)(2,1)} %intensity_in.1) | copy-start | bytes 393220
  5.2 0.8 %copy-start.4 = (f32[128,128]{1,0:T(8,128)S(1)}, f32[128,128]{1,0:T(8,128)}, u32[]{:S(2)}) copy-start(f32[128,128]{1,0:T(8,128)} %phase_in.1) | copy-start | bytes 196612

commit v2 on v1

--- a/solution.py
+++ b/solution.py
@@ -3,8 +3,6 @@
 
 import jax
 import jax.numpy as jnp
-import ml_dtypes
-import numpy as np
 from jax import lax
 from jax.experimental import pallas as pl
 from jax.experimental.pallas import tpu as pltpu
@@ -14,18 +12,19 @@
 SIDE = 128
 HALF = 64
 TILES = 3
+Z_LOW = 4
+Y_SIDE = 4
 
 
 def dft_tables():
-    index = np.arange(SIDE)
-    angles = (index[:, None] * index[None, :] % SIDE) * (-2.0 * math.pi / SIDE)
-    re, im = np.cos(angles) / math.sqrt(SIDE), np.sin(angles) / math.sqrt(SIDE)
-    wide = np.block([[re, im], [-im, re]])
-    parts = []
-    for table in (wide, wide.T):
-        high = table.astype(ml_dtypes.bfloat16)
-        parts += [high, (table - high.astype(np.float64)).astype(ml_dtypes.bfloat16)]
-    return np.stack(parts)
+    rows = lax.broadcasted_iota(jnp.int32, (SIDE, SIDE), 0)
+    lanes = lax.broadcasted_iota(jnp.int32, (SIDE, SIDE), 1)
+    angles = lax.rem(rows * lanes, SIDE).astype(jnp.float32) * (-2.0 * math.pi / SIDE)
+    re, im = jnp.cos(angles) * (1.0 / math.sqrt(SIDE)), jnp.sin(angles) * (1.0 / math.sqrt(SIDE))
+    block = lambda a, b, c, d: jnp.concatenate(
+        [jnp.concatenate([a, b], axis=1), jnp.concatenate([c, d], axis=1)], axis=0
+    )
+    return block(re, im, -im, re), block(re, -im, im, re)
 
 
 def halves(value):
@@ -67,11 +66,11 @@
 
 def kernel(
     rows, cols, total_slots,
-    offsets, counts, trans, probe_in, phase_in, intensity_in, tables_in,
+    offsets, counts, trans, probe_in, phase_in, intensity_in,
     object_out, probe_out,
     ext_first, ext_second, probe, phase, intensity, tables, edge_out, edge_in, patch, wave, prop, place, grid, fold_in, rim_out, rim_in,
-    sum_out, sum_in, col_in, gathered,
-    load_sem, edge_send, edge_recv, row_send, row_recv, fold_send, fold_recv, rim_send, rim_recv, sum_send, sum_recv,
+    sum_out, core_in, plane_out, plane_in, line_in, gathered,
+    load_sem, edge_send, edge_recv, row_send, row_recv, fold_send, fold_recv, rim_send, rim_recv, sum_send, sum_recv, line_sem,
 ):
     ext = (ext_first, ext_second)
     slots = intensity.shape[0]
@@ -94,7 +93,7 @@
     small_loads = [
         pltpu.make_async_copy(src, dst, load_sem.at[4 + i])
         for i, (src, dst) in enumerate(
-            [(phase_in, phase), (probe_in, probe), (tables_in, tables), (intensity_in, intensity)]
+            [(phase_in, phase), (probe_in, probe), (intensity_in, intensity)]
         )
     ]
     for layer in own_loads:
@@ -103,19 +102,48 @@
     for copy in small_loads:
         copy.start()
 
+    x_side, line = rows // (2 * Z_LOW), Z_LOW * (cols // Y_SIDE)
+    plane = x_side * Y_SIDE
+    x, z_low, core = lax.div(row, 2 * Z_LOW), lax.rem(lax.div(row, 2), Z_LOW), lax.rem(row, 2)
+    y, z = lax.rem(col, Y_SIDE), lax.div(col, Y_SIDE) * Z_LOW + z_low
+    spot_in_plane = x * Y_SIDE + y
+
+    def plane_peer(k):
+        to_x = lax.rem(x + lax.div(k, Y_SIDE), x_side)
+        to_y = lax.rem(y + lax.rem(k, Y_SIDE), Y_SIDE)
+        return to_x * Y_SIDE + to_y, {"row": (to_x * Z_LOW + z_low) * 2 + core, "col": col - y + to_y}
+
+    def line_peer(k):
+        to_z = lax.rem(z + k, line)
+        return {"row": (x * Z_LOW + lax.rem(to_z, Z_LOW)) * 2 + core, "col": lax.div(to_z, Z_LOW) * Y_SIDE + y}
+
+    sibling = {"row": row + 1 - 2 * core, "col": col}
+
     barrier = pltpu.get_barrier_semaphore()
 
-    def greet_row(k, _):
-        pl.semaphore_signal(barrier, inc=1, device_id={"row": lax.rem(row + k, rows)}, device_id_type=MESH)
+    def greet(device):
+        pl.semaphore_signal(barrier, inc=1, device_id=device, device_id_type=MESH)
+
+    def greet_plane(k, _):
+        greet(plane_peer(k)[1])
         return 0
 
-    def greet_col(k, _):
-        pl.semaphore_signal(barrier, inc=1, device_id={"col": lax.rem(col + k, cols)}, device_id_type=MESH)
-        return 0
-
-    lax.fori_loop(1, rows, greet_row, 0)
-    lax.fori_loop(1, cols, greet_col, 0)
-    pl.semaphore_wait(barrier, rows + cols - 2)
+    for device in ({"row": up}, {"row": down}, {"col": left}, {"col": right}, line_peer(1), line_peer(line - 1)):
+        greet(device)
+    lax.fori_loop(1, plane, greet_plane, 0)
+
+    reaches = []
+    while 2 ** len(reaches) < line // 2:
+        reaches.append(2 ** len(reaches))
+
+    def line_signal(turn):
+        if turn < len(reaches):
+            for k in (reaches[turn], line - reaches[turn]):
+                pl.semaphore_signal(line_sem.at[turn], inc=1, device_id=line_peer(k), device_id_type=MESH)
+
+    def line_wait(turn):
+        if turn < len(reaches):
+            pl.semaphore_wait(line_sem.at[turn], 2)
 
     def edge_copies(layer):
         return [
@@ -158,8 +186,23 @@
         edge_out[layer, 1] = jnp.where(
             low, ext[layer][0, 0, own, :], pltpu.roll(ext[layer][1, 0, own, :], HALF, 1)
         )
-        start(edge_copies(layer))
-        start(row_copies(layer, 0))
+    pl.semaphore_wait(barrier, plane - 1 + 6)
+    start(edge_copies(0))
+    start(row_copies(0, 0))
+    start(edge_copies(1))
+    line_signal(0)
+
+    for i, table in enumerate(dft_tables()):
+        tables[2 * i], tables[2 * i + 1] = halves(table)
+    for copy in small_loads:
+        copy.wait()
+    prop[0] = jnp.cos(phase[...])
+    prop[1] = jnp.sin(phase[...])
+    place[:, :, :, 0:2, 0:HALF, :] = jnp.zeros(place.shape[:3] + (2, HALF, SIDE), jnp.float32)
+    place[:, :, :, 0:2, 3 * HALF :, :] = jnp.zeros(place.shape[:3] + (2, HALF, SIDE), jnp.float32)
+    place[:, :, :, 2, :, :] = jnp.zeros(place.shape[:3] + (4 * HALF, SIDE), jnp.float32)
+    line_wait(0)
+    line_signal(1)
 
     for layer in range(2):
         landed(edge_copies(layer))
@@ -168,21 +211,17 @@
         ext[layer][0, 2, own, :] = jnp.where(low, from_right, from_left)
         ext[layer][1, 2, own, :] = pltpu.roll(jnp.where(low, from_left, from_right), HALF, 1)
         start(row_copies(layer, 1))
-
-    place[:, :, :, 0:2, 0:HALF, :] = jnp.zeros(place.shape[:3] + (2, HALF, SIDE), jnp.float32)
-    place[:, :, :, 0:2, 3 * HALF :, :] = jnp.zeros(place.shape[:3] + (2, HALF, SIDE), jnp.float32)
-    place[:, :, :, 2, :, :] = jnp.zeros(place.shape[:3] + (4 * HALF, SIDE), jnp.float32)
-    for copy in small_loads:
-        copy.wait()
-    prop[0] = jnp.cos(phase[...])
-    prop[1] = jnp.sin(phase[...])
+        if layer == 0:
+            start(row_copies(1, 0))
+    line_wait(1)
+    line_signal(2)
 
     lanes = lax.broadcasted_iota(jnp.int32, (SIDE, SIDE), 1)
 
     def spot(slot):
-        across = offsets[slot, 1] + (TILES * SIDE - HALF)
+        across = offsets[1, slot] + (TILES * SIDE - HALF)
         tile = lax.rem(lax.div(across, SIDE), TILES)
-        return offsets[slot, 0], tile, lax.rem(tile + 1, TILES), lax.rem(across, SIDE)
+        return offsets[0, slot], tile, lax.rem(tile + 1, TILES), lax.rem(across, SIDE)
 
     spots = [spot(slot) for slot in range(slots)]
 
@@ -283,21 +322,10 @@
         acc = probe_grad[part][:SIDE]
         for slot in range(1, slots):
             acc = acc + probe_grad[part][slot * SIDE : (slot + 1) * SIDE]
-        sum_out[part * SIDE : (part + 1) * SIDE, :] = acc * scale
-    depth = 2 * SIDE // rows
-    piece = lambda k: pl.ds(pl.multiple_of(k * depth, depth), depth)
-
-    def scatter_piece(k):
-        other = lax.rem(row + k, rows)
-        return remote(sum_out.at[piece(other)], sum_in.at[row], sum_send.at[0], sum_recv.at[0], {"row": other})
-
-    def share_piece(k):
-        return remote(col_in.at[col], col_in.at[col], sum_send.at[1], sum_recv.at[1], {"col": lax.rem(col + k, cols)})
-
-    def spread_piece(k):
-        return remote(
-            gathered.at[piece(row)], gathered.at[piece(row)], sum_send.at[2], sum_recv.at[2], {"row": lax.rem(row + k, rows)}
-        )
+        sum_out[part] = acc * scale
+
+    def wait_bytes(ref, sem):
+        pltpu.make_async_copy(ref, ref, sem).wait()
 
     def start_all(copy, count):
         def go(k, _):
@@ -306,23 +334,27 @@
 
         lax.fori_loop(1, count, go, 0)
 
-    def wait_bytes(ref, sem):
-        pltpu.make_async_copy(ref, ref, sem).wait()
-
-    start_all(scatter_piece, rows)
-    scatter(0, times_conj(*back, *shone))
-
-    wait_bytes(sum_in.at[pl.ds(0, rows - 1)], sum_recv.at[0])
-    sum_in[row] = sum_out[piece(row), :]
-    col_in[col] = jnp.sum(sum_in[...], axis=0)
-    start_all(share_piece, cols)
+    halves_in = remote(sum_out.at[1 - core], core_in, sum_send.at[0], sum_recv.at[0], sibling)
+
+    def scatter_piece(k):
+        index, device = plane_peer(k)
+        return remote(plane_out.at[index], plane_in.at[spot_in_plane], sum_send.at[1], sum_recv.at[1], device)
+
+    def share_piece(k):
+        return remote(line_in.at[z], line_in.at[z], sum_send.at[2], sum_recv.at[2], line_peer(k))
+
+    def spread_piece(k):
+        mine = gathered.at[core, spot_in_plane]
+        return remote(mine, mine, sum_send.at[3], sum_recv.at[3], plane_peer(k)[1])
+
+    halves_out = remote(gathered.at[core], gathered.at[core], sum_send.at[4], sum_recv.at[4], sibling)
 
     def fold(layer, tile, part):
         above = jnp.where(row > 0, fold_in[layer, 0, part, tile], 0.0)
         below = jnp.where(row < rows - 1, fold_in[layer, 1, part, tile], 0.0)
         return grid[layer, part, tile, own, :] + above + below
 
-    for layer in (1, 0):
+    def fold_rims(layer):
         landed(fold_copies(layer, 1))
         re, im = fold(layer, 2, 0), fold(layer, 2, 1)
         turned = pltpu.roll(im, HALF, 1)
@@ -330,12 +362,7 @@
         rim_out[layer, 1] = jnp.where(low, turned, re)
         start(rim_copies(layer))
 
-    wait_bytes(col_in.at[pl.ds(0, cols - 1)], sum_recv.at[1])
-    wait_bytes(col_in.at[pl.ds(0, cols - 1)], sum_send.at[1])
-    gathered[piece(row), :] = jnp.sum(col_in[...], axis=0)
-    start_all(spread_piece, rows)
-
-    for layer in (1, 0):
+    def fold_tiles(layer):
         landed(fold_copies(layer, 0))
         landed(rim_copies(layer))
         from_left = jnp.where(col > 0, rim_in[layer, 0], 0.0)
@@ -346,19 +373,38 @@
             object_out[part, layer, :, 0:SIDE] = fold(layer, 0, part) + jnp.where(low, from_left, 0.0)
             object_out[part, layer, :, SIDE:] = fold(layer, 1, part) + jnp.where(low, 0.0, from_right)
 
-    rest = gathered.at[pl.ds(0, depth * (rows - 1))]
-    wait_bytes(rest, sum_recv.at[2])
-    for part in range(2):
-        probe_out[part] = gathered[part * SIDE : (part + 1) * SIDE, :]
-
-    wait_bytes(sum_in.at[pl.ds(0, rows - 1)], sum_send.at[0])
-    wait_bytes(rest, sum_send.at[2])
+    halves_in.start()
+    scatter(0, times_conj(*back, *shone))
+    halves_in.wait_recv()
+    plane_out[...] = (sum_out[core] + core_in[...]).reshape(plane_out.shape)
+    start_all(scatter_piece, plane)
+    plane_in[spot_in_plane] = plane_out[spot_in_plane]
+    fold_rims(1)
+    wait_bytes(plane_in.at[pl.ds(0, plane - 1)], sum_recv.at[1])
+    line_in[z] = jnp.sum(plane_in[...], axis=0)
+    line_wait(2)
+    start_all(share_piece, line)
+    fold_rims(0)
+    fold_tiles(1)
+    wait_bytes(line_in.at[pl.ds(0, line - 1)], sum_recv.at[2])
+    gathered[core, spot_in_plane] = jnp.sum(line_in[...], axis=0)
+    start_all(spread_piece, plane)
+    fold_tiles(0)
+    pieces = gathered.at[core, pl.ds(0, plane - 1)]
+    wait_bytes(pieces, sum_recv.at[3])
+    halves_out.start()
+    halves_in.wait_send()
+    wait_bytes(plane_in.at[pl.ds(0, plane - 1)], sum_send.at[1])
+    wait_bytes(line_in.at[pl.ds(0, line - 1)], sum_send.at[2])
+    wait_bytes(pieces, sum_send.at[3])
     for layer in range(2):
         sent(edge_copies(layer))
         sent(rim_copies(layer))
         for part in range(2):
             sent(row_copies(layer, part))
             sent(fold_copies(layer, part))
+    halves_out.wait()
+    probe_out[...] = gathered[...].reshape(probe_out.shape)
 
 
 def solution(mesh):
@@ -366,10 +412,11 @@
 
     def shards(transmission, probe, prop_phase, intensity, offsets, counts):
         slots = offsets.shape[0]
-        tables = jnp.asarray(dft_tables())
         f32 = jnp.float32
-        depth = 2 * SIDE // rows
-        any_space = pl.BlockSpec(memory_space=pl.ANY)
+        plane = rows // (2 * Z_LOW) * Y_SIDE
+        line = Z_LOW * (cols // Y_SIDE)
+        depth = SIDE // plane
+        hbm = pl.BlockSpec(memory_space=pltpu.HBM)
         smem = pl.BlockSpec(memory_space=pltpu.SMEM)
         vmem = pl.BlockSpec(memory_space=pltpu.VMEM)
         dma = pltpu.SemaphoreType.DMA
@@ -379,7 +426,7 @@
                 jax.ShapeDtypeStruct(transmission.shape, f32),
                 jax.ShapeDtypeStruct(probe.shape, f32),
             ),
-            in_specs=[smem, smem] + [any_space] * 5,
+            in_specs=[smem, smem] + [hbm] * 4,
             out_specs=(vmem, vmem),
             scratch_shapes=[
                 pltpu.VMEM((2, TILES, 3 * HALF, SIDE), f32),
@@ -387,7 +434,7 @@
                 pltpu.VMEM(probe.shape, f32),
                 pltpu.VMEM(prop_phase.shape, f32),
                 pltpu.VMEM(intensity.shape, intensity.dtype),
-                pltpu.VMEM(tables.shape, tables.dtype),
+                pltpu.VMEM((4, 2 * SIDE, 2 * SIDE), jnp.bfloat16),
                 pltpu.VMEM((2, 2, HALF, SIDE), f32),
                 pltpu.VMEM((2, 2, HALF, SIDE), f32),
                 pltpu.VMEM((2, 2, slots * SIDE, SIDE), f32),
@@ -398,11 +445,13 @@
                 pltpu.VMEM((2, 2, 2, TILES, HALF, SIDE), f32),
                 pltpu.VMEM((2, 2, HALF, SIDE), f32),
                 pltpu.VMEM((2, 2, HALF, SIDE), f32),
-                pltpu.VMEM((2 * SIDE, SIDE), f32),
-                pltpu.VMEM((rows, depth, SIDE), f32),
-                pltpu.VMEM((cols, depth, SIDE), f32),
-                pltpu.VMEM((2 * SIDE, SIDE), f32),
-                dma((8,)),
+                pltpu.VMEM((2, SIDE, SIDE), f32),
+                pltpu.VMEM((SIDE, SIDE), f32),
+                pltpu.VMEM((plane, depth, SIDE), f32),
+                pltpu.VMEM((plane, depth, SIDE), f32),
+                pltpu.VMEM((line, depth, SIDE), f32),
+                pltpu.VMEM((2, plane, depth, SIDE), f32),
+                dma((7,)),
                 dma((2, 2)),
                 dma((2, 2)),
                 dma((2, 2, 2)),
@@ -411,13 +460,14 @@
                 dma((2, 2, 2)),
                 dma((2, 2)),
                 dma((2, 2)),
-                dma((3,)),
-                dma((3,)),
+                dma((5,)),
+                dma((5,)),
+                pltpu.SemaphoreType.REGULAR((3,)),
             ],
             compiler_params=pltpu.CompilerParams(
-                collective_id=0, has_side_effects=True, vmem_limit_bytes=40 * 1024 * 1024
-            ),
-        )(offsets, counts, transmission, probe, prop_phase, intensity, tables)
+                collective_id=0, has_side_effects=True, vmem_limit_bytes=60 * 1024 * 1024
+            ),
+        )(offsets.T, counts, transmission, probe, prop_phase, intensity)
 
     in_specs = (
         P(None, None, "row", "col"),

time: 74.6 us -> 68.1 us (0.913)
  local copies, waits for them, and re-layouts: 6.1 us -> 2.37 us
  Pallas kernels: 66.9 us -> 64.3 us
    unnamed x15 -> x4, local copies, waits for them, and re-layouts: 6.1 us -> 2.37 us
    pallas_call x1, Pallas kernels: 66.9 us -> 64.3 us  [shards(): pl.pallas_call(functools.partial(kernel, rows, cols, slots * rows * cols)...]
where the time goes in v2:
time: 68.1 us; the launch traced here: 67.9 us
  Pallas kernels  64.3 us (94%)
  local copies, waits for them, and re-layouts  2.37 us (3%)
  between operations  1.29 us (2%)
    pallas_call x1, Pallas kernels, shards(): pl.pallas_call(functools.partial(kernel, rows, cols, slots * rows * cols)...  64.3 us
    unnamed x4, local copies, waits for them, and re-layouts  2.37 us

profile of v2, /device:TPU:1, one launch (start us, length us, event | category | flops | bytes accessed | tf_op | source)
XLA Modules:
  0.0 67.9 jit_solution(9195188760337224140)
XLA Ops:
  1.3 64.3 %shard_map.77 = (f32[2,2,64,256]{3,2,1,0:T(8,128)}, f32[2,128,128]{2,1,0:T(8,128)}) custom-call(s32[2,4]{1,0:T(2,128)} %bitcast.1, s32[1]{0:T(128)S(6)} %copy.10.counts, f32[2,2,64,256]{3,2,1,0:T(8,128)} %trans.1, f32[2,128,128]{2,1,0:T(8,128)} %probe_in.1, f32[128,128]{1,0:T(8,128)} %phase_in.1, bf16[4,128,128]{2,1,0:T(8,128)(2,1)} %intensity_in.1), custom_call_target="tpu_custom_call" | custom-call | tf_op jit(solution)/shard_map/pallas_call | solution.py:423
  65.5 0.0 copy-start
  65.6 1.7 %copy.11 = f32[2,2,64,256]{3,2,1,0:T(8,128)} copy(f32[2,2,64,256]{3,2,1,0:T(8,128)} %get-tuple-element.4) | data formatting | bytes 524288
  67.3 0.0 copy-done
  67.3 0.7 copy.12
Async XLA Ops:
  65.5 1.7 %copy-start = (f32[2,128,128]{2,1,0:T(8,128)S(1)}, f32[2,128,128]{2,1,0:T(8,128)}, u32[]{:S(2)}) copy-start(f32[2,128,128]{2,1,0:T(8,128)} %get-tuple-element.5) | copy-start | bytes 393220

commit v3 on v2

--- a/solution.py
+++ b/solution.py
@@ -117,7 +117,10 @@
         to_z = lax.rem(z + k, line)
         return {"row": (x * Z_LOW + lax.rem(to_z, Z_LOW)) * 2 + core, "col": lax.div(to_z, Z_LOW) * Y_SIDE + y}
 
-    sibling = {"row": row + 1 - 2 * core, "col": col}
+    def across(device):
+        return {**device, "row": device["row"] + 1 - 2 * core}
+
+    sibling = across({"row": row, "col": col})
 
     barrier = pltpu.get_barrier_semaphore()
 
@@ -126,6 +129,7 @@
 
     def greet_plane(k, _):
         greet(plane_peer(k)[1])
+        greet(across(plane_peer(k)[1]))
         return 0
 
     for device in ({"row": up}, {"row": down}, {"col": left}, {"col": right}, line_peer(1), line_peer(line - 1)):
@@ -186,7 +190,7 @@
         edge_out[layer, 1] = jnp.where(
             low, ext[layer][0, 0, own, :], pltpu.roll(ext[layer][1, 0, own, :], HALF, 1)
         )
-    pl.semaphore_wait(barrier, plane - 1 + 6)
+    pl.semaphore_wait(barrier, 2 * (plane - 1) + 6)
     start(edge_copies(0))
     start(row_copies(0, 0))
     start(edge_copies(1))
@@ -263,7 +267,8 @@
                 grid[layer, part, tile] = total
             if tile == 2:
                 start(fold_copies(layer, 1))
-        start(fold_copies(layer, 0))
+        if layer == 1:
+            start(fold_copies(layer, 0))
 
     def fold_copies(layer, part):
         tiles = slice(0, 2) if part == 0 else slice(2, 3)
@@ -327,12 +332,13 @@
     def wait_bytes(ref, sem):
         pltpu.make_async_copy(ref, ref, sem).wait()
 
-    def start_all(copy, count):
-        def go(k, _):
+    hops = lambda k, count: min(k, count - k)
+    line_order = sorted(range(1, line), key=lambda k: -hops(k, line))
+    plane_order = sorted(range(1, plane), key=lambda k: -hops(k // Y_SIDE, x_side) - hops(k % Y_SIDE, Y_SIDE))
+
+    def start_all(copy, order):
+        for k in order:
             copy(k).start()
-            return 0
-
-        lax.fori_loop(1, count, go, 0)
 
     halves_in = remote(sum_out.at[1 - core], core_in, sum_send.at[0], sum_recv.at[0], sibling)
 
@@ -347,7 +353,9 @@
         mine = gathered.at[core, spot_in_plane]
         return remote(mine, mine, sum_send.at[3], sum_recv.at[3], plane_peer(k)[1])
 
-    halves_out = remote(gathered.at[core], gathered.at[core], sum_send.at[4], sum_recv.at[4], sibling)
+    def spread_across(k):
+        mine = gathered.at[core, spot_in_plane]
+        return remote(mine, mine, sum_send.at[4], sum_recv.at[4], across(plane_peer(k)[1]))
 
     def fold(layer, tile, part):
         above = jnp.where(row > 0, fold_in[layer, 0, part, tile], 0.0)
@@ -377,22 +385,23 @@
     scatter(0, times_conj(*back, *shone))
     halves_in.wait_recv()
     plane_out[...] = (sum_out[core] + core_in[...]).reshape(plane_out.shape)
-    start_all(scatter_piece, plane)
+    start_all(scatter_piece, plane_order)
+    fold_rims(1)
     plane_in[spot_in_plane] = plane_out[spot_in_plane]
-    fold_rims(1)
     wait_bytes(plane_in.at[pl.ds(0, plane - 1)], sum_recv.at[1])
     line_in[z] = jnp.sum(plane_in[...], axis=0)
     line_wait(2)
-    start_all(share_piece, line)
+    start_all(share_piece, line_order)
+    start(fold_copies(0, 0))
     fold_rims(0)
     fold_tiles(1)
     wait_bytes(line_in.at[pl.ds(0, line - 1)], sum_recv.at[2])
     gathered[core, spot_in_plane] = jnp.sum(line_in[...], axis=0)
-    start_all(spread_piece, plane)
+    start_all(spread_piece, plane_order)
+    start_all(spread_across, plane_order + [0])
     fold_tiles(0)
     pieces = gathered.at[core, pl.ds(0, plane - 1)]
     wait_bytes(pieces, sum_recv.at[3])
-    halves_out.start()
     halves_in.wait_send()
     wait_bytes(plane_in.at[pl.ds(0, plane - 1)], sum_send.at[1])
     wait_bytes(line_in.at[pl.ds(0, line - 1)], sum_send.at[2])
@@ -403,7 +412,8 @@
         for part in range(2):
             sent(row_copies(layer, part))
             sent(fold_copies(layer, part))
-    halves_out.wait()
+    wait_bytes(gathered.at[1 - core], sum_recv.at[4])
+    wait_bytes(gathered.at[1 - core], sum_send.at[4])
     probe_out[...] = gathered[...].reshape(probe_out.shape)
 
 

time: 68.1 us -> 62.4 us (0.916)
  Pallas kernels: 64.3 us -> 58.6 us
    pallas_call x1, Pallas kernels: 64.3 us -> 58.6 us  [shards(): pl.pallas_call(functools.partial(kernel, rows, cols, slots * rows * cols)...]
where the time goes in v3:
time: 62.4 us; the launch traced here: 62.2 us
  Pallas kernels  58.6 us (94%)
  local copies, waits for them, and re-layouts  2.37 us (4%)
  between operations  1.29 us (2%)
    pallas_call x1, Pallas kernels, shards(): pl.pallas_call(functools.partial(kernel, rows, cols, slots * rows * cols)...  58.6 us
    unnamed x4, local copies, waits for them, and re-layouts  2.37 us

profile of v3, /device:TPU:1, one launch (start us, length us, event | category | flops | bytes accessed | tf_op | source)
XLA Modules:
  0.0 62.2 jit_solution(12839491857122921541)
XLA Ops:
  1.3 58.6 %shard_map.77 = (f32[2,2,64,256]{3,2,1,0:T(8,128)}, f32[2,128,128]{2,1,0:T(8,128)}) custom-call(s32[2,4]{1,0:T(2,128)} %bitcast.1, s32[1]{0:T(128)S(6)} %copy.10.counts, f32[2,2,64,256]{3,2,1,0:T(8,128)} %trans.1, f32[2,128,128]{2,1,0:T(8,128)} %probe_in.1, f32[128,128]{1,0:T(8,128)} %phase_in.1, bf16[4,128,128]{2,1,0:T(8,128)(2,1)} %intensity_in.1), custom_call_target="tpu_custom_call" | custom-call | tf_op jit(solution)/shard_map/pallas_call | solution.py:433
  59.9 0.0 copy-start
  59.9 1.7 %copy.11 = f32[2,2,64,256]{3,2,1,0:T(8,128)} copy(f32[2,2,64,256]{3,2,1,0:T(8,128)} %get-tuple-element.4) | data formatting | bytes 524288
  61.6 0.0 copy-done
  61.6 0.7 %copy.12 = f32[2,128,128]{2,1,0:T(8,128)} copy(f32[2,128,128]{2,1,0:T(8,128)S(1)} %copy-done) | data formatting | bytes 262144
Async XLA Ops:
  59.9 1.7 %copy-start = (f32[2,128,128]{2,1,0:T(8,128)S(1)}, f32[2,128,128]{2,1,0:T(8,128)}, u32[]{:S(2)}) copy-start(f32[2,128,128]{2,1,0:T(8,128)} %get-tuple-element.5) | copy-start | bytes 393220

commit v4 on v3

--- a/solution.py
+++ b/solution.py
@@ -68,9 +68,9 @@
     rows, cols, total_slots,
     offsets, counts, trans, probe_in, phase_in, intensity_in,
     object_out, probe_out,
-    ext_first, ext_second, probe, phase, intensity, tables, edge_out, edge_in, patch, wave, prop, place, grid, fold_in, rim_out, rim_in,
+    ext_first, ext_second, relay_in, probe, phase, intensity, tables, edge_out, edge_in, patch, wave, prop, place, grid, fold_in, rim_out, rim_in,
     sum_out, core_in, plane_out, plane_in, line_in, gathered,
-    load_sem, edge_send, edge_recv, row_send, row_recv, fold_send, fold_recv, rim_send, rim_recv, sum_send, sum_recv, line_sem,
+    load_sem, edge_send, edge_recv, row_send, row_recv, fold_send, fold_recv, rim_send, rim_recv, sum_send, sum_recv, line_sem, relay_send, relay_recv,
 ):
     ext = (ext_first, ext_second)
     slots = intensity.shape[0]
@@ -169,6 +169,54 @@
             ),
         ]
 
+    depth = HALF // Y_SIDE
+    part_rows = lambda k: pl.ds(pl.multiple_of(k * depth, depth), depth)
+    seams = ((Y_SIDE - 1, 1, lax.rem(col - y + Y_SIDE, cols)), (0, -1, lax.rem(col - y - 1 + cols, cols)))
+
+    def start_spread(turn, copies, out, into, send, recv):
+        for way, (seam, step, _) in enumerate(seams):
+
+            @pl.when(y != seam)
+            def _(way=way):
+                copies[way].start()
+
+            @pl.when(y == seam)
+            def _(way=way, seam=seam, step=step):
+                for k in range(1, Y_SIDE):
+                    device = {"col": col - y + (seam + step * k) % Y_SIDE}
+                    remote(
+                        out.at[way, part_rows(k)], relay_in.at[turn, way], send.at[way], relay_recv.at[turn, way], device
+                    ).start()
+                beyond = {"col": right if way == 0 else left}
+                remote(out.at[way, part_rows(0)], into.at[way, part_rows(0)], send.at[way], recv.at[way], beyond).start()
+
+    def relayed(turn, way, into, recv):
+        seam, _, beyond = seams[way]
+        k = y + 1 if way == 0 else lax.rem(Y_SIDE - y, Y_SIDE)
+        k = lax.rem(k, Y_SIDE)
+        return remote(
+            relay_in.at[turn, way], into.at[way, part_rows(k)], relay_send.at[turn, way], recv.at[way], {"col": beyond}
+        )
+
+    def relay(turn, into, recv):
+        for way, (seam, _, _) in enumerate(seams):
+
+            @pl.when(y != seam)
+            def _(way=way):
+                here = relay_in.at[turn, way]
+                pltpu.make_async_copy(here, here, relay_recv.at[turn, way]).wait()
+                relayed(turn, way, into, recv).start()
+
+    def relay_done(turn, into, recv):
+        for way, (seam, _, _) in enumerate(seams):
+
+            @pl.when(y != seam)
+            def _(way=way):
+                relayed(turn, way, into, recv).wait_send()
+
+    edge_refs = lambda layer: (edge_out.at[layer], edge_in.at[layer], edge_send.at[layer], edge_recv.at[layer])
+    rim_refs = lambda layer: (rim_out.at[layer], rim_in.at[layer], rim_send.at[layer], rim_recv.at[layer])
+
     def start(copies):
         for copy in copies:
             copy.start()
@@ -192,8 +240,8 @@
         )
     pl.semaphore_wait(barrier, 2 * (plane - 1) + 6)
     start(edge_copies(0))
+    start_spread(0, edge_copies(1), *edge_refs(1))
     start(row_copies(0, 0))
-    start(edge_copies(1))
     line_signal(0)
 
     for i, table in enumerate(dft_tables()):
@@ -205,6 +253,7 @@
     place[:, :, :, 0:2, 0:HALF, :] = jnp.zeros(place.shape[:3] + (2, HALF, SIDE), jnp.float32)
     place[:, :, :, 0:2, 3 * HALF :, :] = jnp.zeros(place.shape[:3] + (2, HALF, SIDE), jnp.float32)
     place[:, :, :, 2, :, :] = jnp.zeros(place.shape[:3] + (4 * HALF, SIDE), jnp.float32)
+    relay(0, *edge_refs(1)[1::2])
     line_wait(0)
     line_signal(1)
 
@@ -368,7 +417,7 @@
         turned = pltpu.roll(im, HALF, 1)
         rim_out[layer, 0] = jnp.where(low, re, turned)
         rim_out[layer, 1] = jnp.where(low, turned, re)
-        start(rim_copies(layer))
+        start_spread(2 - layer, rim_copies(layer), *rim_refs(layer))
 
     def fold_tiles(layer):
         landed(fold_copies(layer, 0))
@@ -387,6 +436,7 @@
     plane_out[...] = (sum_out[core] + core_in[...]).reshape(plane_out.shape)
     start_all(scatter_piece, plane_order)
     fold_rims(1)
+    relay(1, *rim_refs(1)[1::2])
     plane_in[spot_in_plane] = plane_out[spot_in_plane]
     wait_bytes(plane_in.at[pl.ds(0, plane - 1)], sum_recv.at[1])
     line_in[z] = jnp.sum(plane_in[...], axis=0)
@@ -395,6 +445,7 @@
     start(fold_copies(0, 0))
     fold_rims(0)
     fold_tiles(1)
+    relay(2, *rim_refs(0)[1::2])
     wait_bytes(line_in.at[pl.ds(0, line - 1)], sum_recv.at[2])
     gathered[core, spot_in_plane] = jnp.sum(line_in[...], axis=0)
     start_all(spread_piece, plane_order)
@@ -406,6 +457,9 @@
     wait_bytes(plane_in.at[pl.ds(0, plane - 1)], sum_send.at[1])
     wait_bytes(line_in.at[pl.ds(0, line - 1)], sum_send.at[2])
     wait_bytes(pieces, sum_send.at[3])
+    relay_done(0, *edge_refs(1)[1::2])
+    relay_done(1, *rim_refs(1)[1::2])
+    relay_done(2, *rim_refs(0)[1::2])
     for layer in range(2):
         sent(edge_copies(layer))
         sent(rim_copies(layer))
@@ -441,6 +495,7 @@
             scratch_shapes=[
                 pltpu.VMEM((2, TILES, 3 * HALF, SIDE), f32),
                 pltpu.VMEM((2, TILES, 3 * HALF, SIDE), f32),
+                pltpu.VMEM((3, 2, HALF // Y_SIDE, SIDE), f32),
                 pltpu.VMEM(probe.shape, f32),
                 pltpu.VMEM(prop_phase.shape, f32),
                 pltpu.VMEM(intensity.shape, intensity.dtype),
@@ -473,6 +528,8 @@
                 dma((5,)),
                 dma((5,)),
                 pltpu.SemaphoreType.REGULAR((3,)),
+                dma((3, 2)),
+                dma((3, 2)),
             ],
             compiler_params=pltpu.CompilerParams(
                 collective_id=0, has_side_effects=True, vmem_limit_bytes=60 * 1024 * 1024

time: 62.4 us -> 59.9 us (0.960)
  Pallas kernels: 58.6 us -> 56.1 us
    pallas_call x1, Pallas kernels: 58.6 us -> 56.1 us  [shards(): pl.pallas_call(functools.partial(kernel, rows, cols, slots * rows * cols)...]
where the time goes in v4:
time: 59.9 us; the launch traced here: 59.7 us
  Pallas kernels  56.1 us (94%)
  local copies, waits for them, and re-layouts  2.37 us (4%)
  between operations  1.29 us (2%)
    pallas_call x1, Pallas kernels, shards(): pl.pallas_call(functools.partial(kernel, rows, cols, slots * rows * cols)...  56.1 us
    unnamed x4, local copies, waits for them, and re-layouts  2.37 us

profile of v4, /device:TPU:1, one launch (start us, length us, event | category | flops | bytes accessed | tf_op | source)
XLA Modules:
  0.0 59.7 jit_solution(14006627029516592372)
XLA Ops:
  1.3 56.1 %shard_map.77 = (f32[2,2,64,256]{3,2,1,0:T(8,128)}, f32[2,128,128]{2,1,0:T(8,128)}) custom-call(s32[2,4]{1,0:T(2,128)} %bitcast.1, s32[1]{0:T(128)S(6)} %copy.10.counts, f32[2,2,64,256]{3,2,1,0:T(8,128)} %trans.1, f32[2,128,128]{2,1,0:T(8,128)} %probe_in.1, f32[128,128]{1,0:T(8,128)} %phase_in.1, bf16[4,128,128]{2,1,0:T(8,128)(2,1)} %intensity_in.1), custom_call_target="tpu_custom_call" | custom-call | tf_op jit(solution)/shard_map/pallas_call | solution.py:487
  57.3 0.0 copy-start
  57.4 1.7 %copy.11 = f32[2,2,64,256]{3,2,1,0:T(8,128)} copy(f32[2,2,64,256]{3,2,1,0:T(8,128)} %get-tuple-element.4) | data formatting | bytes 524288
  59.1 0.0 copy-done
  59.1 0.7 %copy.12 = f32[2,128,128]{2,1,0:T(8,128)} copy(f32[2,128,128]{2,1,0:T(8,128)S(1)} %copy-done) | data formatting | bytes 262144
Async XLA Ops:
  57.3 1.7 %copy-start = (f32[2,128,128]{2,1,0:T(8,128)S(1)}, f32[2,128,128]{2,1,0:T(8,128)}, u32[]{:S(2)}) copy-start(f32[2,128,128]{2,1,0:T(8,128)} %get-tuple-element.5) | copy-start | bytes 393220

commit v5 on v4

--- a/solution.py
+++ b/solution.py
@@ -69,8 +69,8 @@
     offsets, counts, trans, probe_in, phase_in, intensity_in,
     object_out, probe_out,
     ext_first, ext_second, relay_in, probe, phase, intensity, tables, edge_out, edge_in, patch, wave, prop, place, grid, fold_in, rim_out, rim_in,
-    sum_out, core_in, plane_out, plane_in, line_in, gathered,
-    load_sem, edge_send, edge_recv, row_send, row_recv, fold_send, fold_recv, rim_send, rim_recv, sum_send, sum_recv, line_sem, relay_send, relay_recv,
+    result, sum_out, plane_in, line_in, gathered,
+    load_sem, store_sem, edge_send, edge_recv, row_send, row_recv, fold_send, fold_recv, rim_send, rim_recv, sum_send, sum_recv, line_sem, relay_send, relay_recv,
 ):
     ext = (ext_first, ext_second)
     slots = intensity.shape[0]
@@ -96,44 +96,41 @@
             [(phase_in, phase), (probe_in, probe), (intensity_in, intensity)]
         )
     ]
+    x_side, line = rows // (2 * Z_LOW), Z_LOW * (cols // Y_SIDE)
+    plane = x_side * Y_SIDE
+    x, z_low, core = lax.div(row, 2 * Z_LOW), lax.rem(lax.div(row, 2), Z_LOW), lax.rem(row, 2)
+    y, z = lax.rem(col, Y_SIDE), lax.div(col, Y_SIDE) * Z_LOW + z_low
+    spot_in_plane = x * Y_SIDE + y
+
+    def plane_peer(k):
+        to_x = lax.rem(x + lax.div(k, Y_SIDE), x_side)
+        to_y = lax.rem(y + lax.rem(k, Y_SIDE), Y_SIDE)
+        return to_x * Y_SIDE + to_y, {"row": (to_x * Z_LOW + z_low) * 2 + core, "col": col - y + to_y}
+
+    def line_peer(k):
+        to_z = lax.rem(z + k, line)
+        return {"row": (x * Z_LOW + lax.rem(to_z, Z_LOW)) * 2 + core, "col": lax.div(to_z, Z_LOW) * Y_SIDE + y}
+
+    def across(device):
+        return {**device, "row": device["row"] + 1 - 2 * core}
+
+    barrier = pltpu.get_barrier_semaphore()
+
+    def greet(device):
+        pl.semaphore_signal(barrier, inc=1, device_id=device, device_id_type=MESH)
+
+    def greet_plane(k, _):
+        greet(plane_peer(k)[1])
+        greet(across(plane_peer(k)[1]))
+        return 0
+
+    for device in ({"row": up}, {"row": down}, {"col": left}, {"col": right}, line_peer(1), line_peer(line - 1)):
+        greet(device)
     for layer in own_loads:
         for copy in layer:
             copy.start()
     for copy in small_loads:
         copy.start()
-
-    x_side, line = rows // (2 * Z_LOW), Z_LOW * (cols // Y_SIDE)
-    plane = x_side * Y_SIDE
-    x, z_low, core = lax.div(row, 2 * Z_LOW), lax.rem(lax.div(row, 2), Z_LOW), lax.rem(row, 2)
-    y, z = lax.rem(col, Y_SIDE), lax.div(col, Y_SIDE) * Z_LOW + z_low
-    spot_in_plane = x * Y_SIDE + y
-
-    def plane_peer(k):
-        to_x = lax.rem(x + lax.div(k, Y_SIDE), x_side)
-        to_y = lax.rem(y + lax.rem(k, Y_SIDE), Y_SIDE)
-        return to_x * Y_SIDE + to_y, {"row": (to_x * Z_LOW + z_low) * 2 + core, "col": col - y + to_y}
-
-    def line_peer(k):
-        to_z = lax.rem(z + k, line)
-        return {"row": (x * Z_LOW + lax.rem(to_z, Z_LOW)) * 2 + core, "col": lax.div(to_z, Z_LOW) * Y_SIDE + y}
-
-    def across(device):
-        return {**device, "row": device["row"] + 1 - 2 * core}
-
-    sibling = across({"row": row, "col": col})
-
-    barrier = pltpu.get_barrier_semaphore()
-
-    def greet(device):
-        pl.semaphore_signal(barrier, inc=1, device_id=device, device_id_type=MESH)
-
-    def greet_plane(k, _):
-        greet(plane_peer(k)[1])
-        greet(across(plane_peer(k)[1]))
-        return 0
-
-    for device in ({"row": up}, {"row": down}, {"col": left}, {"col": right}, line_peer(1), line_peer(line - 1)):
-        greet(device)
     lax.fori_loop(1, plane, greet_plane, 0)
 
     reaches = []
@@ -376,7 +373,7 @@
         acc = probe_grad[part][:SIDE]
         for slot in range(1, slots):
             acc = acc + probe_grad[part][slot * SIDE : (slot + 1) * SIDE]
-        sum_out[part] = acc * scale
+        sum_out[part] = (acc * scale).reshape(sum_out.shape[1:])
 
     def wait_bytes(ref, sem):
         pltpu.make_async_copy(ref, ref, sem).wait()
@@ -389,27 +386,32 @@
         for k in order:
             copy(k).start()
 
-    halves_in = remote(sum_out.at[1 - core], core_in, sum_send.at[0], sum_recv.at[0], sibling)
-
     def scatter_piece(k):
         index, device = plane_peer(k)
-        return remote(plane_out.at[index], plane_in.at[spot_in_plane], sum_send.at[1], sum_recv.at[1], device)
+        return remote(sum_out.at[core, index], plane_in.at[from_here], sum_send.at[0], sum_recv.at[0], device)
+
+    def scatter_across(k):
+        index, device = plane_peer(k)
+        return remote(sum_out.at[1 - core, index], plane_in.at[from_here], sum_send.at[0], sum_recv.at[0], across(device))
 
     def share_piece(k):
-        return remote(line_in.at[z], line_in.at[z], sum_send.at[2], sum_recv.at[2], line_peer(k))
+        return remote(line_in.at[z], line_in.at[z], sum_send.at[1], sum_recv.at[1], line_peer(k))
 
     def spread_piece(k):
         mine = gathered.at[core, spot_in_plane]
-        return remote(mine, mine, sum_send.at[3], sum_recv.at[3], plane_peer(k)[1])
+        return remote(mine, mine, sum_send.at[2], sum_recv.at[2], plane_peer(k)[1])
 
     def spread_across(k):
         mine = gathered.at[core, spot_in_plane]
-        return remote(mine, mine, sum_send.at[4], sum_recv.at[4], across(plane_peer(k)[1]))
+        return remote(mine, mine, sum_send.at[3], sum_recv.at[3], across(plane_peer(k)[1]))
 
     def fold(layer, tile, part):
         above = jnp.where(row > 0, fold_in[layer, 0, part, tile], 0.0)
         below = jnp.where(row < rows - 1, fold_in[layer, 1, part, tile], 0.0)
         return grid[layer, part, tile, own, :] + above + below
+
+    def store(layer):
+        return pltpu.make_async_copy(result.at[layer], object_out.at[:, layer], store_sem.at[layer])
 
     def fold_rims(layer):
         landed(fold_copies(layer, 1))
@@ -427,18 +429,18 @@
         for part in range(2):
             if part == 1:
                 from_left, from_right = pltpu.roll(from_left, HALF, 1), pltpu.roll(from_right, HALF, 1)
-            object_out[part, layer, :, 0:SIDE] = fold(layer, 0, part) + jnp.where(low, from_left, 0.0)
-            object_out[part, layer, :, SIDE:] = fold(layer, 1, part) + jnp.where(low, 0.0, from_right)
-
-    halves_in.start()
+            result[layer, part, :, 0:SIDE] = fold(layer, 0, part) + jnp.where(low, from_left, 0.0)
+            result[layer, part, :, SIDE:] = fold(layer, 1, part) + jnp.where(low, 0.0, from_right)
+        store(layer).start()
+
+    from_here = core * plane + spot_in_plane
+    start_all(scatter_piece, plane_order)
+    start_all(scatter_across, plane_order + [0])
     scatter(0, times_conj(*back, *shone))
-    halves_in.wait_recv()
-    plane_out[...] = (sum_out[core] + core_in[...]).reshape(plane_out.shape)
-    start_all(scatter_piece, plane_order)
     fold_rims(1)
     relay(1, *rim_refs(1)[1::2])
-    plane_in[spot_in_plane] = plane_out[spot_in_plane]
-    wait_bytes(plane_in.at[pl.ds(0, plane - 1)], sum_recv.at[1])
+    plane_in[from_here] = sum_out[core, spot_in_plane]
+    wait_bytes(plane_in.at[pl.ds(0, 2 * plane - 1)], sum_recv.at[0])
     line_in[z] = jnp.sum(plane_in[...], axis=0)
     line_wait(2)
     start_all(share_piece, line_order)
@@ -446,17 +448,16 @@
     fold_rims(0)
     fold_tiles(1)
     relay(2, *rim_refs(0)[1::2])
-    wait_bytes(line_in.at[pl.ds(0, line - 1)], sum_recv.at[2])
+    wait_bytes(line_in.at[pl.ds(0, line - 1)], sum_recv.at[1])
     gathered[core, spot_in_plane] = jnp.sum(line_in[...], axis=0)
     start_all(spread_piece, plane_order)
     start_all(spread_across, plane_order + [0])
     fold_tiles(0)
     pieces = gathered.at[core, pl.ds(0, plane - 1)]
-    wait_bytes(pieces, sum_recv.at[3])
-    halves_in.wait_send()
-    wait_bytes(plane_in.at[pl.ds(0, plane - 1)], sum_send.at[1])
-    wait_bytes(line_in.at[pl.ds(0, line - 1)], sum_send.at[2])
-    wait_bytes(pieces, sum_send.at[3])
+    wait_bytes(pieces, sum_recv.at[2])
+    wait_bytes(plane_in.at[pl.ds(0, 2 * plane - 1)], sum_send.at[0])
+    wait_bytes(line_in.at[pl.ds(0, line - 1)], sum_send.at[1])
+    wait_bytes(pieces, sum_send.at[2])
     relay_done(0, *edge_refs(1)[1::2])
     relay_done(1, *rim_refs(1)[1::2])
     relay_done(2, *rim_refs(0)[1::2])
@@ -466,9 +467,27 @@
         for part in range(2):
             sent(row_copies(layer, part))
             sent(fold_copies(layer, part))
-    wait_bytes(gathered.at[1 - core], sum_recv.at[4])
-    wait_bytes(gathered.at[1 - core], sum_send.at[4])
-    probe_out[...] = gathered[...].reshape(probe_out.shape)
+    wait_bytes(gathered.at[1 - core], sum_recv.at[3])
+    wait_bytes(gathered.at[1 - core], sum_send.at[3])
+    store_sum = pltpu.make_async_copy(gathered, probe_out, store_sem.at[2])
+    store_sum.start()
+    store(0).wait()
+    store(1).wait()
+    store_sum.wait()
+
+
+def deliver(object_in, probe_in, object_out, probe_out, object_held, probe_held, sem):
+    parts = [(object_in.at[i, j], object_held.at[i, j], object_out.at[i, j]) for i in range(2) for j in range(2)]
+    parts += [(probe_in.at[i], probe_held.at[i], probe_out.at[i]) for i in range(2)]
+    loads = [pltpu.make_async_copy(src, held, sem.at[0, i]) for i, (src, held, _) in enumerate(parts)]
+    stores = [pltpu.make_async_copy(held, dst, sem.at[1, i]) for i, (_, held, dst) in enumerate(parts)]
+    for load in loads:
+        load.start()
+    for load, store in zip(loads, stores):
+        load.wait()
+        store.start()
+    for store in stores:
+        store.wait()
 
 
 def solution(mesh):
@@ -482,16 +501,15 @@
         depth = SIDE // plane
         hbm = pl.BlockSpec(memory_space=pltpu.HBM)
         smem = pl.BlockSpec(memory_space=pltpu.SMEM)
-        vmem = pl.BlockSpec(memory_space=pltpu.VMEM)
         dma = pltpu.SemaphoreType.DMA
-        return pl.pallas_call(
+        outs = pl.pallas_call(
             functools.partial(kernel, rows, cols, slots * rows * cols),
             out_shape=(
                 jax.ShapeDtypeStruct(transmission.shape, f32),
-                jax.ShapeDtypeStruct(probe.shape, f32),
+                jax.ShapeDtypeStruct((2, plane, depth, SIDE), f32),
             ),
             in_specs=[smem, smem] + [hbm] * 4,
-            out_specs=(vmem, vmem),
+            out_specs=(hbm, hbm),
             scratch_shapes=[
                 pltpu.VMEM((2, TILES, 3 * HALF, SIDE), f32),
                 pltpu.VMEM((2, TILES, 3 * HALF, SIDE), f32),
@@ -510,13 +528,13 @@
                 pltpu.VMEM((2, 2, 2, TILES, HALF, SIDE), f32),
                 pltpu.VMEM((2, 2, HALF, SIDE), f32),
                 pltpu.VMEM((2, 2, HALF, SIDE), f32),
-                pltpu.VMEM((2, SIDE, SIDE), f32),
-                pltpu.VMEM((SIDE, SIDE), f32),
-                pltpu.VMEM((plane, depth, SIDE), f32),
-                pltpu.VMEM((plane, depth, SIDE), f32),
+                pltpu.VMEM((2, 2, HALF, 2 * SIDE), f32),
+                pltpu.VMEM((2, plane, depth, SIDE), f32),
+                pltpu.VMEM((2 * plane, depth, SIDE), f32),
                 pltpu.VMEM((line, depth, SIDE), f32),
                 pltpu.VMEM((2, plane, depth, SIDE), f32),
                 dma((7,)),
+                dma((3,)),
                 dma((2, 2)),
                 dma((2, 2)),
                 dma((2, 2, 2)),
@@ -525,8 +543,8 @@
                 dma((2, 2, 2)),
                 dma((2, 2)),
                 dma((2, 2)),
-                dma((5,)),
-                dma((5,)),
+                dma((4,)),
+                dma((4,)),
                 pltpu.SemaphoreType.REGULAR((3,)),
                 dma((3, 2)),
                 dma((3, 2)),
@@ -535,6 +553,17 @@
                 collective_id=0, has_side_effects=True, vmem_limit_bytes=60 * 1024 * 1024
             ),
         )(offsets.T, counts, transmission, probe, prop_phase, intensity)
+        return pl.pallas_call(
+            deliver,
+            out_shape=(
+                jax.ShapeDtypeStruct(transmission.shape, f32),
+                jax.ShapeDtypeStruct(probe.shape, f32),
+            ),
+            in_specs=[hbm, hbm],
+            out_specs=(hbm, hbm),
+            scratch_shapes=[pltpu.VMEM(transmission.shape, f32), pltpu.VMEM(probe.shape, f32), dma((2, 6))],
+            compiler_params=pltpu.CompilerParams(vmem_limit_bytes=60 * 1024 * 1024),
+        )(outs[0], outs[1].reshape(probe.shape))
 
     in_specs = (
         P(None, None, "row", "col"),

time: 59.9 us -> 58.8 us (0.982)
  local copies, waits for them, and re-layouts: 2.37 us -> 0 us
  Pallas kernels: 56.1 us -> 57.3 us
    unnamed x4 -> x0, local copies, waits for them, and re-layouts: 2.37 us -> none
    pallas_call x0 -> x1, Pallas kernels: none -> 1.73 us  [shards(): pl.pallas_call(deliver, out_shape=(jax.ShapeDtypeStruct(transmission.shap...]
where the time goes in v5:
time: 58.8 us; the launch traced here: 58.5 us
  Pallas kernels  57.3 us (97%)
  between operations  1.29 us (2%)
    pallas_call x1, Pallas kernels, shards(): pl.pallas_call(functools.partial(kernel, rows, cols, slots * rows * cols)...  55.5 us
    pallas_call x1, Pallas kernels, shards(): pl.pallas_call(deliver, out_shape=(jax.ShapeDtypeStruct(transmission.shap...  1.73 us

profile of v5, /device:TPU:1, one launch (start us, length us, event | category | flops | bytes accessed | tf_op | source)
XLA Modules:
  0.0 58.5 jit_solution(17773359990609530846)
XLA Ops:
  1.3 55.5 %shard_map.77 = (f32[2,2,64,256]{3,2,1,0:T(8,128)}, f32[2,16,8,128]{3,2,1,0:T(8,128)}) custom-call(s32[2,4]{1,0:T(2,128)} %bitcast.3, s32[1]{0:T(128)S(6)} %copy.8.counts, f32[2,2,64,256]{3,2,1,0:T(8,128)} %trans.1, f32[2,128,128]{2,1,0:T(8,128)} %probe_in.1, f32[128,128]{1,0:T(8,128)} %phase_in.1, bf16[4,128,128]{2,1,0:T(8,128)(2,1)} %intensity_in.1), custom_call_target="tpu_custom_call" | custom-call | tf_op jit(solution)/shard_map/pallas_call | solution.py:505
  56.8 1.7 %shard_map.78 = (f32[2,2,64,256]{3,2,1,0:T(8,128)}, f32[2,128,128]{2,1,0:T(8,128)}) custom-call(f32[2,2,64,256]{3,2,1,0:T(8,128)} %get-tuple-element.4.object_in, f32[2,128,128]{2,1,0:T(8,128)} %bitcast.2), custom_call_target="tpu_custom_call" | custom-call | tf_op jit(solution)/shard_map/pallas_call | solution.py:556

commit v6 on v5

--- a/solution.py
+++ b/solution.py
@@ -226,7 +226,7 @@
         for copy in copies:
             copy.wait_send()
 
-    for layer in range(2):
+    def pack(layer):
         for copy in own_loads[layer]:
             copy.wait()
         edge_out[layer, 0] = jnp.where(
@@ -235,11 +235,15 @@
         edge_out[layer, 1] = jnp.where(
             low, ext[layer][0, 0, own, :], pltpu.roll(ext[layer][1, 0, own, :], HALF, 1)
         )
+
+    pack(0)
     pl.semaphore_wait(barrier, 2 * (plane - 1) + 6)
     start(edge_copies(0))
+    pack(1)
     start_spread(0, edge_copies(1), *edge_refs(1))
     start(row_copies(0, 0))
     line_signal(0)
+    relay(0, *edge_refs(1)[1::2])
 
     for i, table in enumerate(dft_tables()):
         tables[2 * i], tables[2 * i + 1] = halves(table)
@@ -250,7 +254,6 @@
     place[:, :, :, 0:2, 0:HALF, :] = jnp.zeros(place.shape[:3] + (2, HALF, SIDE), jnp.float32)
     place[:, :, :, 0:2, 3 * HALF :, :] = jnp.zeros(place.shape[:3] + (2, HALF, SIDE), jnp.float32)
     place[:, :, :, 2, :, :] = jnp.zeros(place.shape[:3] + (4 * HALF, SIDE), jnp.float32)
-    relay(0, *edge_refs(1)[1::2])
     line_wait(0)
     line_signal(1)
 
@@ -455,22 +458,22 @@
     fold_tiles(0)
     pieces = gathered.at[core, pl.ds(0, plane - 1)]
     wait_bytes(pieces, sum_recv.at[2])
+    wait_bytes(gathered.at[1 - core], sum_recv.at[3])
+    store_sum = pltpu.make_async_copy(gathered, probe_out, store_sem.at[2])
+    store_sum.start()
     wait_bytes(plane_in.at[pl.ds(0, 2 * plane - 1)], sum_send.at[0])
     wait_bytes(line_in.at[pl.ds(0, line - 1)], sum_send.at[1])
     wait_bytes(pieces, sum_send.at[2])
+    wait_bytes(gathered.at[1 - core], sum_send.at[3])
+    relay_done(2, *rim_refs(0)[1::2])
+    relay_done(1, *rim_refs(1)[1::2])
     relay_done(0, *edge_refs(1)[1::2])
-    relay_done(1, *rim_refs(1)[1::2])
-    relay_done(2, *rim_refs(0)[1::2])
     for layer in range(2):
         sent(edge_copies(layer))
         sent(rim_copies(layer))
         for part in range(2):
             sent(row_copies(layer, part))
             sent(fold_copies(layer, part))
-    wait_bytes(gathered.at[1 - core], sum_recv.at[3])
-    wait_bytes(gathered.at[1 - core], sum_send.at[3])
-    store_sum = pltpu.make_async_copy(gathered, probe_out, store_sem.at[2])
-    store_sum.start()
     store(0).wait()
     store(1).wait()
     store_sum.wait()

time: 58.8 us -> 58.7 us (level)
  no operation moved by 1% of the time
where the time goes in v6:
time: 58.7 us; the launch traced here: 58.5 us
  Pallas kernels  57.2 us (97%)
  between operations  1.29 us (2%)
    pallas_call x1, Pallas kernels, shards(): pl.pallas_call(functools.partial(kernel, rows, cols, slots * rows * cols)...  55.5 us
    pallas_call x1, Pallas kernels, shards(): pl.pallas_call(deliver, out_shape=(jax.ShapeDtypeStruct(transmission.shap...  1.73 us

profile of v6, /device:TPU:1, one launch (start us, length us, event | category | flops | bytes accessed | tf_op | source)
XLA Modules:
  0.0 58.5 jit_solution(12693335850444285016)
XLA Ops:
  1.3 55.5 %shard_map.77 = (f32[2,2,64,256]{3,2,1,0:T(8,128)}, f32[2,16,8,128]{3,2,1,0:T(8,128)}) custom-call(s32[2,4]{1,0:T(2,128)} %bitcast.3, s32[1]{0:T(128)S(6)} %copy.8.counts, f32[2,2,64,256]{3,2,1,0:T(8,128)} %trans.1, f32[2,128,128]{2,1,0:T(8,128)} %probe_in.1, f32[128,128]{1,0:T(8,128)} %phase_in.1, bf16[4,128,128]{2,1,0:T(8,128)(2,1)} %intensity_in.1), custom_call_target="tpu_custom_call" | custom-call | tf_op jit(solution)/shard_map/pallas_call | solution.py:508
  56.8 1.7 %shard_map.78 = (f32[2,2,64,256]{3,2,1,0:T(8,128)}, f32[2,128,128]{2,1,0:T(8,128)}) custom-call(f32[2,2,64,256]{3,2,1,0:T(8,128)} %get-tuple-element.4.object_in, f32[2,128,128]{2,1,0:T(8,128)} %bitcast.2), custom_call_target="tpu_custom_call" | custom-call | tf_op jit(solution)/shard_map/pallas_call | solution.py:559
